TPU v7x, 32 devices: a whole 2x2x4 slice. The times are simulated.
32 devices in a mesh: section: 4 (over x, core), expert: 8 (over z, y).
Axes of the slice: x: 2, y: 2, z: 4, core: 2. Of those that a mesh axis runs over, the one named last changes fastest.
Arguments:
- activations: bfloat16 [2, 2048, 5120], P(None, ('section', 'expert')), may hold values from -20 to 20
- norm_gain: float32 [5120], replicated, may hold values from 0.1 to 1.9
- router_weight: bfloat16 [5120, 32], P(None, ('section', 'expert')), may hold values from -0.078125 to 0.078125
- gate_proj: bfloat16 [4, 8, 768, 5120], P(None, 'expert', 'section'), may hold values from -0.078125 to 0.078125
- up_proj: bfloat16 [4, 8, 768, 5120], P(None, 'expert', 'section'), may hold values from -0.078125 to 0.078125
- down_proj: bfloat16 [4, 8, 768, 5120], P(None, 'expert', 'section'), may hold values from -0.21875 to 0.21875
- expert_ids: int32 [2, 2048, 2], P(None, ('section', 'expert')), may hold values from 0 to 31, all different within a row; in each aligned block of 64 rows (0 to 63, 64 to 127, ..., all dimensions but the last counted through in order) at most 8 rows name the same one
Outputs:
- mixture: bfloat16 [2, 2048, 5120], P(None, ('section', 'expert'))
Inputs may be any that keep to these rules, and one draw needn't show every extreme that they name: `expert_ids`: in the rows of one device at one step (aligned blocks of 64 sequences), no expert is named more than 8 times, a bound that some block reaches; each row names 2 different experts.
All inputs are finite; a program needn't handle non-finite values.
Results may differ from a plain program's by a relative error of at most 0.0074.
Values may be sent and summed in bfloat16 or wider, within the bound.
No kernel may reach another device: no remote copies, remote signals or barrier semaphores. Data moves between devices by JAX's collectives and lax.ppermute only.
A program may use at most 192 MiB of HBM per device.

v0:
```python
import jax
import jax.numpy as jnp
from jax import lax
from jax.sharding import PartitionSpec as P

epsilon = 1e-05
contract = (((1,), (1,)), ((), ()))


def expert_apply(inputs, gate_matrix, up_matrix, down_matrix, router_column):
    gate_part = lax.dot_general(inputs, gate_matrix, contract, preferred_element_type=jnp.float32)
    up_part = lax.dot_general(inputs, up_matrix, contract, preferred_element_type=jnp.float32)
    hidden = (jax.nn.silu(gate_part) * up_part).astype(jnp.bfloat16)
    result = jnp.dot(hidden, down_matrix, preferred_element_type=jnp.float32)
    logits = jnp.dot(inputs, router_column, preferred_element_type=jnp.float32)[:, 0]
    return (result, jax.nn.sigmoid(logits))


def dispatch(outgoing, counts):
    incoming, got_counts = (
        lax.all_to_all(outgoing, ("section", "expert"), split_axis=0, concat_axis=0, tiled=True),
        lax.all_to_all(counts, ("section", "expert"), split_axis=0, concat_axis=0, tiled=True),
    )
    return (incoming, got_counts)


def combine(returned, scores):
    back_rows, back_scores = (
        lax.all_to_all(returned, ("section", "expert"), split_axis=0, concat_axis=0, tiled=True),
        lax.all_to_all(scores, ("section", "expert"), split_axis=0, concat_axis=0, tiled=True),
    )
    return (back_rows, back_scores)


def on_device(activations, norm_gain, router_weight, gate_proj, up_proj, down_proj, expert_ids):
    synced = (
        lax.all_to_all(gate_proj, "section", split_axis=0, concat_axis=2, tiled=True),
        lax.all_to_all(up_proj, "section", split_axis=0, concat_axis=2, tiled=True),
        lax.all_to_all(down_proj, "section", split_axis=0, concat_axis=2, tiled=True),
    )
    model_width = activations.shape[2]
    gate_matrix = synced[0].reshape(-1, model_width)
    up_matrix = synced[1].reshape(-1, model_width)
    down_matrix = synced[2].reshape(-1, model_width)
    section_count = lax.axis_size("section")
    expert_count = lax.axis_size("expert")
    experts = section_count * expert_count
    top_count = expert_ids.shape[2]
    capacity = max(2, 2 * top_count * activations.shape[1] // experts)
    expert_range = jnp.arange(experts, dtype=jnp.int32)
    outputs = []
    for step_index in range(activations.shape[0]):
        current = activations[step_index].astype(jnp.float32)
        inverse_rms = lax.rsqrt(jnp.mean(current * current, axis=1, keepdims=True) + epsilon)
        normed = (current * inverse_rms * norm_gain).astype(jnp.bfloat16)
        chosen = expert_ids[step_index].reshape(-1)
        pick_count = chosen.shape[0]
        positions = jnp.arange(pick_count, dtype=jnp.int32)
        same_expert = chosen[:, None] == chosen[None, :]
        earlier = positions[:, None] > positions[None, :]
        slot_index = jnp.sum(jnp.logical_and(same_expert, earlier).astype(jnp.int32), axis=1)
        source_rows = jnp.repeat(normed, top_count, axis=0)
        outgoing = (
            jnp.zeros((experts, capacity, model_width), jnp.bfloat16)
            .at[chosen, slot_index]
            .set(source_rows)
        )
        counts = jnp.sum((chosen[:, None] == expert_range[None, :]).astype(jnp.float32), axis=0)[
            :, None
        ].astype(jnp.bfloat16)
        incoming, got_counts = dispatch(outgoing, counts)
        live_slots = jnp.arange(capacity, dtype=jnp.float32)[None, :] < got_counts.astype(
            jnp.float32
        )
        flat_input = incoming.reshape(experts * capacity, model_width)
        flat_live = live_slots.reshape(-1)
        result, gate_score = expert_apply(
            flat_input, gate_matrix, up_matrix, down_matrix, router_weight
        )
        live_mask = flat_live.astype(jnp.float32)
        returned = (
            (result * live_mask[:, None])
            .astype(jnp.bfloat16)
            .reshape(experts, capacity, model_width)
        )
        scores = (gate_score * live_mask).astype(jnp.bfloat16).reshape(experts, capacity)
        back_rows, back_scores = combine(returned, scores)
        picked = (
            back_rows[chosen, slot_index].astype(jnp.float32).reshape(-1, top_count, model_width)
        )
        weights = back_scores[chosen, slot_index].astype(jnp.float32).reshape(-1, top_count)
        mixture_rows = jnp.sum(picked * weights[:, :, None], axis=1) / jnp.sum(
            weights, axis=1, keepdims=True
        )
        outputs.append(mixture_rows.astype(jnp.bfloat16))
    return jnp.stack(outputs)


def solution(mesh):
    return jax.shard_map(
        on_device,
        mesh=mesh,
        in_specs=(
            P(None, ("section", "expert"), None),
            P(),
            P(None, ("section", "expert")),
            P(None, "expert", "section", None),
            P(None, "expert", "section", None),
            P(None, "expert", "section", None),
            P(None, ("section", "expert"), None),
        ),
        out_specs=P(None, ("section", "expert"), None),
        check_vma=False,
    )
```

profile of v0, /device:TPU:0, one launch (start us, length us, event | category | flops | bytes accessed | tf_op | source)
XLA Modules:
  0.0 649.0 jit_solution(14522262533313615512)
XLA Ops:
  1.8 7.3 %all-to-all-start.4 = ((bf16[32,1,1]{2,1,0:T(2,128)(2,1)}), bf16[32,1,1]{2,1,0:T(2,128)(2,1)S(1)}, u32[]{:S(2)}, u32[]{:S(2)}) async-start(bf16[32,1,1]{2,1,0:T(2,128)(2,1)} %copy.51), calls=%async_computation.4 | async-start | bytes 32768 | tf_op jit(solution)/shard_map/all_to_all | solution.py:22
  16.2 4.7 all-to-all-start.8
  20.9 1.8 broadcast.173.clone
  22.7 38.7 %scatter_fusion.1 = bf16[32,8,5120]{2,1,0:T(8,128)(2,1)} fusion(bf16[32,8,5120]{2,1,0:T(8,128)(2,1)} %broadcast.173.clone, s32[128]{0:T(128)S(1)} %get-tuple-element.9, bf16[128,5120]{1,0:T(8,128)(2,1)S(1)} %reshape.412), kind=kCustom, calls=%fused_computation.5 | custom fusion | bytes 3933184 | tf_op jit(solution)/shard_map/scatter | solution.py:66
  61.4 5.9 all-to-all-start.7
  68.9 1.8 broadcast.173.clone.1
  70.7 38.6 %scatter_fusion = bf16[32,8,5120]{2,1,0:T(8,128)(2,1)} fusion(bf16[32,8,5120]{2,1,0:T(8,128)(2,1)} %broadcast.173.clone.1, s32[128]{0:T(128)S(1)} %get-tuple-element.7, bf16[128,5120]{1,0:T(8,128)(2,1)S(1)} %reshape.406), kind=kCustom, calls=%fused_computation.4 | custom fusion | bytes 3933184 | tf_op jit(solution)/shard_map/scatter | solution.py:66
  109.3 19.6 %all-to-all-done.7 = bf16[32,8,5120]{2,1,0:T(8,128)(2,1)} async-done(((bf16[32,8,5120]{2,1,0:T(8,128)(2,1)}), bf16[32,8,5120]{2,1,0:T(8,128)(2,1)}, u32[]{:S(2)}, u32[]{:S(2)}) %all-to-all-start.7) | async-done | bytes 2621472 | tf_op jit(solution)/shard_map/all_to_all | solution.py:21
  128.9 3.7 all-to-all-start
  133.0 7.6 %fusion.40 = f32[1,32,8]{2,0,1:T(1,128)S(1)} fusion(bf16[32,8,5120]{2,1,0:T(8,128)(2,1)} %all-to-all-done.7, bf16[5120,1]{0,1:T(2,128)(2,1)S(1)} %copy-done), kind=kOutput, calls=%fused_computation.48 | convolution fusion | flops 2621440 | bytes 2632704 | tf_op jit(solution)/shard_map/dot_general | solution.py:15
  140.7 53.4 %all-to-all-done = bf16[32,8,5120]{2,1,0:T(8,128)(2,1)} async-done(((bf16[32,8,5120]{2,1,0:T(8,128)(2,1)}), bf16[32,8,5120]{2,1,0:T(8,128)(2,1)}, u32[]{:S(2)}, u32[]{:S(2)}) %all-to-all-start) | async-done | bytes 2621472 | tf_op jit(solution)/shard_map/all_to_all | solution.py:21
  194.2 9.4 %all_to_all.77 = bf16[32,1,8]{2,1,0:T(2,128)(2,1)S(1)} all-to-all(bf16[32,1,8]{2,1,0:T(2,128)(2,1)S(1)} %copy.59), channel_id=1, replica_groups=mesh['section'=4,'expert'=8] {'section','expert'}, dimensions={0} | all-to-all | bytes 1024 | tf_op jit(solution)/shard_map/all_to_all | solution.py:30
  203.5 94.8 %all_to_all.78 = bf16[4,1,192,5120]{3,2,1,0:T(8,128)(2,1)} all-to-all(bf16[4,1,192,5120]{3,2,1,0:T(8,128)(2,1)} %param.10), channel_id=1, replica_groups=mesh['section'=4,'expert'=8] {'section'}, dimensions={0} | all-to-all | bytes 15728640 | tf_op jit(solution)/shard_map/all_to_all | solution.py:37
  298.4 94.8 %all_to_all.79 = bf16[4,1,192,5120]{3,2,1,0:T(8,128)(2,1)} all-to-all(bf16[4,1,192,5120]{3,2,1,0:T(8,128)(2,1)} %param.11), channel_id=1, replica_groups=mesh['section'=4,'expert'=8] {'section'}, dimensions={0} | all-to-all | bytes 15728640 | tf_op jit(solution)/shard_map/all_to_all | solution.py:38
  393.2 5.5 all-to-all-start.3
  399.3 7.6 %fusion.42 = f32[1,32,8]{2,0,1:T(1,128)S(1)} fusion(bf16[32,8,5120]{2,1,0:T(8,128)(2,1)} %all-to-all-done, bf16[5120,1]{0,1:T(2,128)(2,1)S(1)} %copy-done), kind=kOutput, calls=%fused_computation.50 | convolution fusion | flops 2621440 | bytes 2632704 | tf_op jit(solution)/shard_map/dot_general | solution.py:15
  407.6 6.3 fusion.6
  413.9 72.4 %all-to-all-done.3 = bf16[4,1,192,5120]{3,2,1,0:T(8,128)(2,1)} async-done(((bf16[4,1,192,5120]{3,2,1,0:T(8,128)(2,1)}), bf16[4,1,192,5120]{3,2,1,0:T(8,128)(2,1)}, u32[]{:S(2)}, u32[]{:S(2)}) %all-to-all-start.3) | async-done | bytes 7864352 | tf_op jit(solution)/shard_map/all_to_all | solution.py:39
  486.3 2.9 all-to-all-start.6
  489.3 13.2 %fusion.2 = bf16[32,8,5120]{2,1,0:T(8,128)(2,1)} fusion(bf16[768,5120]{1,0:T(8,128)(2,1)} %bitcast.7, f32[256]{0:T(256)S(1)} %reshape.377, bf16[768,5120]{1,0:T(8,128)(2,1)} %bitcast.126, bf16[32,8,5120]{2,1,0:T(8,128)(2,1)} %all-to-all-done.7, f32[256,768]{1,0:T(8,128)S(1)} %fusion.6), kind=kOutput, calls=%fused_computation.10 | convolution fusion | flops 4030332928 | bytes 21758976 | tf_op jit(solution)/shard_map/dot_general | solution.py:14
  502.5 5.9 all-to-all-start.9
  508.6 6.3 fusion.10
  514.9 13.1 %fusion.3 = bf16[32,8,5120]{2,1,0:T(8,128)(2,1)} fusion(bf16[768,5120]{1,0:T(8,128)(2,1)} %bitcast.7, f32[256]{0:T(256)S(1)} %reshape.372, bf16[768,5120]{1,0:T(8,128)(2,1)} %bitcast.127, bf16[32,8,5120]{2,1,0:T(8,128)(2,1)} %all-to-all-done, f32[256,768]{1,0:T(8,128)S(1)} %fusion.10), kind=kOutput, calls=%fused_computation.11 | convolution fusion | flops 4030332928 | bytes 21758976 | tf_op jit(solution)/shard_map/dot_general | solution.py:14
  528.0 42.0 %all-to-all-done.9 = bf16[32,8,5120]{2,1,0:T(8,128)(2,1)S(1)} async-done(((bf16[32,8,5120]{2,1,0:T(8,128)(2,1)}), bf16[32,8,5120]{2,1,0:T(8,128)(2,1)S(1)}, u32[]{:S(2)}, u32[]{:S(2)}) %all-to-all-start.9) | async-done | bytes 2621472 | tf_op jit(solution)/shard_map/all_to_all | solution.py:29
  570.1 3.7 all-to-all-start.5
  577.4 5.7 gather_fusion.2
  583.1 3.0 reshape.378
  586.1 4.6 multiply_reduce_fusion
  590.8 44.5 %all-to-all-done.5 = bf16[32,8,5120]{2,1,0:T(8,128)(2,1)} async-done(((bf16[32,8,5120]{2,1,0:T(8,128)(2,1)}), bf16[32,8,5120]{2,1,0:T(8,128)(2,1)}, u32[]{:S(2)}, u32[]{:S(2)}) %all-to-all-start.5) | async-done | bytes 2621472 | tf_op jit(solution)/shard_map/all_to_all | solution.py:29
  635.3 5.4 gather_fusion
  640.7 3.0 reshape.373
  643.7 3.6 multiply_reduce_fusion.1
  (56 shorter events, 17.5 us)
Async XLA Ops:
  0.0 132.9 %copy-start = (bf16[5120,1]{0,1:T(2,128)(2,1)S(1)}, bf16[5120,1]{0,1:T(2,128)(2,1)}, u32[]{:S(2)}) copy-start(bf16[5120,1]{0,1:T(2,128)(2,1)} %param.9) | copy-start | bytes 30724
  1.8 14.4 %all-to-all-start.4 = ((bf16[32,1,1]{2,1,0:T(2,128)(2,1)}), bf16[32,1,1]{2,1,0:T(2,128)(2,1)S(1)}, u32[]{:S(2)}, u32[]{:S(2)}) async-start(bf16[32,1,1]{2,1,0:T(2,128)(2,1)} %copy.51), calls=%async_computation.4 | async-start | bytes 32768 | tf_op jit(solution)/shard_map/all_to_all | solution.py:22
  16.2 45.2 %all-to-all-start.8 = ((bf16[32,1,1]{2,1,0:T(2,128)(2,1)}), bf16[32,1,1]{2,1,0:T(2,128)(2,1)S(1)}, u32[]{:S(2)}, u32[]{:S(2)}) async-start(bf16[32,1,1]{2,1,0:T(2,128)(2,1)} %copy.57), calls=%async_computation.8 | async-start | bytes 32768 | tf_op jit(solution)/shard_map/all_to_all | solution.py:22
  61.4 67.5 %all-to-all-start.7 = ((bf16[32,8,5120]{2,1,0:T(8,128)(2,1)}), bf16[32,8,5120]{2,1,0:T(8,128)(2,1)}, u32[]{:S(2)}, u32[]{:S(2)}) async-start(bf16[32,8,5120]{2,1,0:T(8,128)(2,1)} %scatter_fusion.1), calls=%async_computation.7 | async-start | bytes 5242880 | tf_op jit(solution)/shard_map/all_to_all | solution.py:21
  128.9 65.2 %all-to-all-start = ((bf16[32,8,5120]{2,1,0:T(8,128)(2,1)}), bf16[32,8,5120]{2,1,0:T(8,128)(2,1)}, u32[]{:S(2)}, u32[]{:S(2)}) async-start(bf16[32,8,5120]{2,1,0:T(8,128)(2,1)} %scatter_fusion), calls=%async_computation | async-start | bytes 5242880 | tf_op jit(solution)/shard_map/all_to_all | solution.py:21
  393.2 93.1 %all-to-all-start.3 = ((bf16[4,1,192,5120]{3,2,1,0:T(8,128)(2,1)}), bf16[4,1,192,5120]{3,2,1,0:T(8,128)(2,1)}, u32[]{:S(2)}, u32[]{:S(2)}) async-start(bf16[4,1,192,5120]{3,2,1,0:T(8,128)(2,1)} %param.12), calls=%async_computation.3 | async-start | bytes 15728640 | tf_op jit(solution)/shard_map/all_to_all | solution.py:39
  486.3 16.2 %all-to-all-start.6 = ((bf16[32,1,8]{2,1,0:T(2,128)(2,1)}), bf16[32,1,8]{2,1,0:T(2,128)(2,1)S(1)}, u32[]{:S(2)}, u32[]{:S(2)}) async-start(bf16[32,1,8]{2,1,0:T(2,128)(2,1)} %copy.53), calls=%async_computation.6 | async-start | bytes 32768 | tf_op jit(solution)/shard_map/all_to_all | solution.py:30
  502.5 67.6 %all-to-all-start.9 = ((bf16[32,8,5120]{2,1,0:T(8,128)(2,1)}), bf16[32,8,5120]{2,1,0:T(8,128)(2,1)S(1)}, u32[]{:S(2)}, u32[]{:S(2)}) async-start(bf16[32,8,5120]{2,1,0:T(8,128)(2,1)} %fusion.2), calls=%async_computation.9 | async-start | bytes 5242880 | tf_op jit(solution)/shard_map/all_to_all | solution.py:29
  570.1 65.2 %all-to-all-start.5 = ((bf16[32,8,5120]{2,1,0:T(8,128)(2,1)}), bf16[32,8,5120]{2,1,0:T(8,128)(2,1)}, u32[]{:S(2)}, u32[]{:S(2)}) async-start(bf16[32,8,5120]{2,1,0:T(8,128)(2,1)} %fusion.3), calls=%async_computation.5 | async-start | bytes 5242880 | tf_op jit(solution)/shard_map/all_to_all | solution.py:29
  643.7 3.6 copy-start.2
  647.3 1.5 copy-start.1
where the time goes:
time: 658 us; the launch traced here: 649 us
  waiting for transfers between devices  233 us (35%)
  blocking collectives  199 us (30%)
  local copies, waits for them, and re-layouts  108 us (16%)
  matrix products  54 us (8%)
  starting transfers between devices  39.7 us (6%)
  other arithmetic  14.5 us (2%)
    all_to_all x1, blocking collectives, on_device(): lax.all_to_all(up_proj, 'section', split_axis=0, concat_axis=2, tiled=True)  94.8 us
    all_to_all x1, blocking collectives, on_device(): lax.all_to_all(gate_proj, 'section', split_axis=0, concat_axis=2, tiled=T...  94.8 us
    all_to_all x2, waiting for transfers between devices, combine(): lax.all_to_all(returned, ('section', 'expert'), split_axis=0, concat_axis...  86.6 us
    scatter x2, local copies, waits for them, and re-layouts, on_device(): outgoing = jnp.zeros((experts, capacity, model_width), jnp.bfloat16).at[c...  77.3 us
    all_to_all x2, waiting for transfers between devices, dispatch(): lax.all_to_all(outgoing, ('section', 'expert'), split_axis=0, concat_axis...  73 us
    all_to_all x1, waiting for transfers between devices, on_device(): lax.all_to_all(down_proj, 'section', split_axis=0, concat_axis=2, tiled=T...  72.4 us
    dot_general x2, matrix products, expert_apply(): result = jnp.dot(hidden, down_matrix, preferred_element_type=jnp.float32)  26.4 us
    dot_general x2, matrix products, expert_apply(): jnp.dot(inputs, router_column, preferred_element_type=jnp.float32)[:, 0]  15.1 us
  transfers between devices with their start and end apart: 8, of which 6 were waited for; matrix products, arithmetic and copies ran while one was open for 25% of the time, Pallas kernels for 0%

commit v1 on v0

v1 whole, which is shorter than its diff:
```python
import jax
import jax.numpy as jnp
from jax import lax
from jax.sharding import Mesh, PartitionSpec as P

epsilon = 1e-05
contract = (((1,), (1,)), ((), ()))
swap = [(0, 1), (1, 0)]
group = ("core", "expert")


def side_swap(values):
    return lax.ppermute(values, "side", swap)


def core_swap(values):
    return lax.ppermute(values, "core", swap)


def cross_swap(values):
    return lax.ppermute(values, ("side", "core"), [(0, 3), (1, 2), (2, 1), (3, 0)])


def normalise(rows, norm_gain):
    current = rows.astype(jnp.float32)
    inverse_rms = lax.rsqrt(jnp.mean(current * current, axis=1, keepdims=True) + epsilon)
    return (current * inverse_rms * norm_gain).astype(jnp.bfloat16)


def on_device(activations, norm_gain, router_weight, gate_proj, up_proj, down_proj, expert_ids):
    steps, rows, width = activations.shape
    top = expert_ids.shape[2]
    columns = lax.axis_size("expert")
    cores = lax.axis_size("core")
    local = gate_proj.shape[0] // cores
    experts = gate_proj.shape[0] * columns
    capacity = max(2, 2 * top * rows // experts)
    part = gate_proj.shape[2]
    half = width // 2
    side = lax.axis_index("side")
    core = lax.axis_index("core")
    peers = cores * columns

    pack, member = [], []
    for step in range(steps):
        named = jnp.any(
            expert_ids[step][:, :, None] == jnp.arange(experts, dtype=jnp.int32), axis=1
        )
        count = named.astype(jnp.int32)
        earlier = jnp.cumsum(count, axis=0) - count
        taken = named[:, :, None] & (earlier[:, :, None] == jnp.arange(capacity, dtype=jnp.int32))
        taken = taken.reshape(rows, cores, local, columns, capacity)
        pack.append(
            [
                taken[:, :, i].reshape(rows, peers * capacity).T.astype(jnp.bfloat16)
                for i in range(local)
            ]
        )
        member.append(named)

    normed = [normalise(activations[step], norm_gain) for step in range(steps)]

    router_rows = lax.all_gather(
        router_weight.reshape(1, width), ("side", "core", "expert"), axis=0, tiled=True
    )

    gate_up, down_near, down_far = [], [], []
    for i in range(local):
        mine, theirs = core * local + i, (1 - core) * local + i

        def expert_of(weights, index):
            return lax.dynamic_index_in_dim(weights, index, 0, keepdims=False)[0]

        def down_block(index, which):
            return lax.dynamic_slice(
                down_proj, (index, 0, 0, which * half), (1, 1, part, half)
            ).reshape(part, half)

        gate_up.append(
            jnp.concatenate(
                [
                    expert_of(gate_proj, mine),
                    core_swap(expert_of(gate_proj, theirs)),
                    expert_of(up_proj, mine),
                    core_swap(expert_of(up_proj, theirs)),
                ],
                axis=0,
            )
        )
        down_near.append(
            jnp.concatenate([down_block(mine, side), core_swap(down_block(theirs, side))], axis=0)
        )
        down_far.append(
            jnp.concatenate(
                [
                    side_swap(down_block(mine, 1 - side)),
                    cross_swap(down_block(theirs, 1 - side)),
                ],
                axis=0,
            )
        )

    scatter, total = [], []
    for step in range(steps):
        logits = lax.dot_general(
            normed[step], router_rows, contract, preferred_element_type=jnp.float32
        )
        score = jnp.where(member[step], jax.nn.sigmoid(logits).astype(jnp.bfloat16), 0)
        by_slot = score.reshape(rows, cores, local, columns)
        own = jnp.stack(
            [
                pack[step][i].T.reshape(rows, peers, capacity)
                * by_slot[:, :, i].reshape(rows, peers, 1)
                for i in range(local)
            ]
        )
        other = side_swap(own)
        zeros = jnp.zeros_like(own)
        both = jnp.concatenate(
            [jnp.stack([own, zeros], axis=3), jnp.stack([zeros, other], axis=3)], axis=1
        )
        scatter.append(both.reshape(local, 2 * rows, peers * 2 * capacity))
        total.append(
            jnp.sum(both.astype(jnp.float32), axis=(0, 2, 3, 4)).reshape(2 * rows, 1)
        )

    numerators = [0.0] * steps
    for i in range(local):
        for step in range(steps):
            outgoing = jnp.dot(pack[step][i], normed[step]).reshape(peers, capacity, width)
            near = lax.all_to_all(outgoing, group, split_axis=0, concat_axis=0, tiled=True)
            far = side_swap(near)
            inputs = jnp.stack([near, far], axis=1).reshape(-1, width)
            products = lax.dot_general(
                inputs, gate_up[i], contract, preferred_element_type=jnp.float32
            )
            gate_part, up_part = jnp.split(products, 2, axis=1)
            hidden = (jax.nn.silu(gate_part) * up_part).astype(jnp.bfloat16)
            units = hidden.shape[1]
            other_hidden = side_swap(
                jnp.flip(hidden.reshape(peers, 2, capacity, units), axis=1).reshape(-1, units)
            )
            result = jnp.dot(
                jnp.concatenate([hidden, other_hidden], axis=1),
                jnp.concatenate([down_near[i], down_far[i]], axis=0),
                preferred_element_type=jnp.float32,
            ).astype(jnp.bfloat16)
            returned = lax.all_to_all(
                result.reshape(peers, 2 * capacity, half),
                group,
                split_axis=0,
                concat_axis=0,
                tiled=True,
            ).reshape(-1, half)
            numerators[step] += jnp.dot(
                scatter[step][i], returned, preferred_element_type=jnp.float32
            )

    outputs = []
    for step in range(steps):
        mixture = (numerators[step] / total[step]).astype(jnp.bfloat16)
        own, received = mixture[:rows], side_swap(mixture[rows:])
        low = jnp.where(side == 0, own, received)
        high = jnp.where(side == 0, received, own)
        outputs.append(jnp.concatenate([low, high], axis=1))
    return jnp.stack(outputs)


def solution(mesh):
    sections, columns = mesh.shape["section"], mesh.shape["expert"]
    split = Mesh(mesh.devices.reshape(2, sections // 2, columns), ("side", "core", "expert"))
    everywhere = ("side", "core", "expert")
    weights = P(None, "expert", ("side", "core"), None)
    return jax.shard_map(
        on_device,
        mesh=split,
        in_specs=(
            P(None, everywhere, None),
            P(),
            P(None, everywhere),
            weights,
            weights,
            weights,
            P(None, everywhere, None),
        ),
        out_specs=P(None, everywhere, None),
        check_vma=False,
    )
```

time: 658 us -> 448 us (0.68); the launches traced: 649 us -> 447 us
  blocking collectives: 199 us -> 73.2 us
  local copies, waits for them, and re-layouts: 108 us -> 28.1 us
  waiting for transfers between devices: 233 us -> 200 us
  starting transfers between devices: 39.7 us -> 58.9 us
  matrix products: 54 us -> 65.2 us
    all_to_all x3 -> x0, blocking collectives: 199 us -> none  [the longest x1 94.8 us: on_device(): lax.all_to_all(up_proj, 'section', split_axis=0, concat_axis=2, tiled=True)]
    all_to_all x8, waiting for transfers between devices: 233 us -> 90.3 us  [the longest x4 59.8 us: on_device(): lax.all_to_all(outgoing, group, split_axis=0, concat_axis=0, tiled=True)]
    ppermute x0 -> x22, waiting for transfers between devices: none -> 110 us  [the longest x14 84.6 us: side_swap(): return lax.ppermute(values, 'side', swap)]
    scatter x2 -> x0, local copies, waits for them, and re-layouts: 77.3 us -> none  [on_device(): outgoing = jnp.zeros((experts, capacity, model_width), jnp.bfloat16).at[c...]
    all_gather x0 -> x1, blocking collectives: none -> 73.2 us  [on_device(): lax.all_gather(router_weight.reshape(1, width), ('side', 'core', 'expert'...]
    ppermute x0 -> x22, starting transfers between devices: none -> 21.7 us  [the longest x14 20.5 us: side_swap(): return lax.ppermute(values, 'side', swap)]
    gather x4 -> x0, local copies, waits for them, and re-layouts: 14.1 us -> none  [the longest x2 11.1 us: on_device(): back_rows[chosen, slot_index].astype(jnp.float32)]
    squeeze x0 -> x2, local copies, waits for them, and re-layouts: none -> 13.2 us  [expert_of(): return lax.dynamic_index_in_dim(weights, index, 0, keepdims=False)[0]]
  transfers between devices with their start and end apart: 8 -> 30, of which waited for: 6 -> 13; matrix products, arithmetic and copies ran while one was open for 25% -> 23% of each run, Pallas kernels for 0% -> 0%
where the time goes in v1:
time: 448 us; the launch traced here: 447 us
  waiting for transfers between devices  200 us (45%)
  blocking collectives  73.2 us (16%)
  matrix products  65.2 us (15%)
  starting transfers between devices  58.9 us (13%)
  local copies, waits for them, and re-layouts  28.1 us (6%)
  other arithmetic  20.1 us (4%)
    ppermute x14, waiting for transfers between devices, side_swap(): return lax.ppermute(values, 'side', swap)  84.6 us
    all_gather x1, blocking collectives, on_device(): lax.all_gather(router_weight.reshape(1, width), ('side', 'core', 'expert'...  73.2 us
    all_to_all x4, waiting for transfers between devices, on_device(): lax.all_to_all(outgoing, group, split_axis=0, concat_axis=0, tiled=True)  59.8 us
    dot_general x4, matrix products, on_device(): lax.dot_general(inputs, gate_up[i], contract, preferred_element_type=jnp....  34.6 us
    all_to_all x4, waiting for transfers between devices, on_device(): lax.all_to_all(result.reshape(peers, 2 * capacity, half), group, split_ax...  30.5 us
    ppermute x2, waiting for transfers between devices, cross_swap(): lax.ppermute(values, ('side', 'core'), [(0, 3), (1, 2), (2, 1), (3, 0)])  25.4 us
    ppermute x14, starting transfers between devices, side_swap(): return lax.ppermute(values, 'side', swap)  20.5 us
    all_to_all x4, starting transfers between devices, on_device(): lax.all_to_all(outgoing, group, split_axis=0, concat_axis=0, tiled=True)  20.1 us
  transfers between devices with their start and end apart: 30, of which 13 were waited for; matrix products, arithmetic and copies ran while one was open for 23% of the time, Pallas kernels for 0%

profile of v1, /device:TPU:0, one launch (start us, length us, event | category | flops | bytes accessed | tf_op | source)
XLA Modules:
  0.0 446.5 jit_solution(15036204170521459647)
XLA Ops:
  5.4 7.4 %all-to-all-start.2 = ((bf16[16,8,5120]{2,1,0:T(8,128)(2,1)}), bf16[16,8,5120]{2,1,0:T(8,128)(2,1)}, u32[]{:S(2)}, u32[]{:S(2)}) async-start(bf16[16,8,5120]{2,1,0:T(8,128)(2,1)} %fusion.74), calls=%async_computation.2 | async-start | bytes 2621440 | tf_op jit(solution)/shard_map/all_to_all | solution.py:131
  14.5 30.2 %all-to-all-done.2 = bf16[16,8,5120]{2,1,0:T(8,128)(2,1)} async-done(((bf16[16,8,5120]{2,1,0:T(8,128)(2,1)}), bf16[16,8,5120]{2,1,0:T(8,128)(2,1)}, u32[]{:S(2)}, u32[]{:S(2)}) %all-to-all-start.2) | async-done | bytes 1310752 | tf_op jit(solution)/shard_map/all_to_all | solution.py:131
  44.7 4.4 all-to-all-start
  51.2 29.6 %all-to-all-done = bf16[16,8,5120]{2,1,0:T(8,128)(2,1)} async-done(((bf16[16,8,5120]{2,1,0:T(8,128)(2,1)}), bf16[16,8,5120]{2,1,0:T(8,128)(2,1)}, u32[]{:S(2)}, u32[]{:S(2)}) %all-to-all-start) | async-done | bytes 1310752 | tf_op jit(solution)/shard_map/all_to_all | solution.py:131
  80.8 3.7 all-to-all-start.6
  84.5 6.6 %dynamic-slice_bitcast_fusion.1 = (bf16[192,5120]{1,0:T(8,128)(2,1)}, bf16[192,5120]{1,0:T(8,128)(2,1)}, bf16[192,5120]{1,0:T(8,128)(2,1)}, bf16[192,5120]{1,0:T(8,128)(2,1)}) fusion(bf16[4,1,192,5120]{3,2,1,0:T(8,128)(2,1)} %param.11, s32[]{:T(128)S(6)} %select_n.70, s32[]{:T(128)S(6)} %select_n.67, s32[]{:T(128)S(6)} %select_n.66, s32[]{:T(128)S(6)} %select_n.71), kind=kLoop, calls=%fused_computation.19 | loop fusion | bytes 15728656 | tf_op jit(solution)/shard_map/squeeze | solution.py:72
  91.5 6.6 %dynamic-slice_bitcast_fusion.3 = (bf16[192,5120]{1,0:T(8,128)(2,1)}, bf16[192,5120]{1,0:T(8,128)(2,1)}, bf16[192,5120]{1,0:T(8,128)(2,1)}, bf16[192,5120]{1,0:T(8,128)(2,1)}) fusion(bf16[4,1,192,5120]{3,2,1,0:T(8,128)(2,1)} %param.10, s32[]{:T(128)S(6)} %select_n.70, s32[]{:T(128)S(6)} %select_n.67, s32[]{:T(128)S(6)} %select_n.66, s32[]{:T(128)S(6)} %select_n.71), kind=kLoop, calls=%fused_computation.21 | loop fusion | bytes 15728656 | tf_op jit(solution)/shard_map/squeeze | solution.py:72
  99.7 6.5 %dynamic-slice_bitcast_fusion.11 = (bf16[192,2560]{1,0:T(8,128)(2,1)}, bf16[192,2560]{1,0:T(8,128)(2,1)}, bf16[192,2560]{1,0:T(8,128)(2,1)}, bf16[192,2560]{1,0:...) fusion(bf16[4,1,192,5120]{3,2,1,0:T(8,128)(2,1)} %param.12, ...), kind=kLoop, calls=%fused_computation.64 | loop fusion | bytes 15728664 | tf_op jit(solution)/shard_map/reshape | solution.py:77
  106.8 73.2 %all-gather = bf16[163840,1]{0,1:T(2,128)(2,1)S(1)} all-gather(bf16[5120,1]{0,1:T(2,128)(2,1)S(1)} %copy-done.13), channel_id=2, replica_groups=mesh['side'=2,'core'=2,'expert'=8] {'side','core','expert'}, dimensions={0}, use_global_device_ids=true | all-gather | bytes 337920 | tf_op jit(solution)/shard_map/all_gather | solution.py:63
  180.1 7.5 %reduce = bf16[163840]{0:T(1024)(128)(2,1)} reduce(bf16[163840,1]{0,1:T(2,128)(2,1)S(1)} %all-gather, bf16[]{:T(256)} %constant.83), dimensions={1}, to_apply=%all-gather.reduce_sub_computation | reduce | bytes 655362 | tf_op jit(solution)/shard_map/all_gather | solution.py:63
  190.4 4.6 %all-to-all-start.4 = ((bf16[16,8,5120]{2,1,0:T(8,128)(2,1)}), bf16[16,8,5120]{2,1,0:T(8,128)(2,1)}, u32[]{:S(2)}, u32[]{:S(2)}) async-start(bf16[16,8,5120]{2,1,0:T(8,128)(2,1)} %fusion.80), calls=%async_computation.4 | async-start | bytes 2621440 | tf_op jit(solution)/shard_map/all_to_all | solution.py:131
  199.3 8.6 %fusion.9 = f32[256,768]{1,0:T(8,128)S(1)} fusion(bf16[256,5120]{1,0:T(8,128)(2,1)S(1)} %bitcast.171, bf16[192,5120]{1,0:T(8,128)(2,1)} %collective-permute-done.10, bf16[192,5120]{1,0:T(8,128)(2,1)S(1)} %copy-done.1, bf16[192,5120]{1,0:T(8,128)(2,1)} %collective-permute-done.9, bf16[192,5120]{1,0:T(8,128)(2,1)S(1)} %copy-done.3), kind=kOutput, calls=%fused_computation.35 | convolution fusion | flops 2044723200 | bytes 11272192 | tf_op jit(solution)/shard_map/dot_general | solution.py:134
  209.1 5.6 %collective-permute-done.14 = bf16[192,2560]{1,0:T(8,128)(2,1)} collective-permute-done((bf16[192,2560]{1,0:T(8,128)(2,1)}, bf16[192,2560]{1,0:T(8,128)(2,1)}, u32[]{:S(2)}, u32[]{:S(2)}) %collective-permute-start.14) | collective-permute-done | bytes 983072 | tf_op jit(solution)/shard_map/ppermute | solution.py:21
  214.7 30.4 %collective-permute-done.11 = bf16[256,384]{1,0:T(8,128)(2,1)S(1)} collective-permute-done((bf16[256,384]{1,0:T(8,128)(2,1)S(1)}, bf16[256,384]{1,0:T(8,128)(2,1)S(1)}, u32[]{:S(2)}, u32[]{:S(2)}) %collective-permute-start.11) | collective-permute-done | bytes 196640 | tf_op jit(solution)/shard_map/ppermute | solution.py:13
  247.4 4.3 convolution_convert_fusion.2
  251.8 4.4 all-to-all-start.3
  260.3 8.6 %fusion.11 = f32[256,768]{1,0:T(8,128)S(1)} fusion(bf16[256,5120]{1,0:T(8,128)(2,1)S(1)} %bitcast.172, bf16[192,5120]{1,0:T(8,128)(2,1)} %collective-permute-done.3, bf16[192,5120]{1,0:T(8,128)(2,1)S(1)} %copy-done.5, bf16[192,5120]{1,0:T(8,128)(2,1)} %collective-permute-done.2, bf16[192,5120]{1,0:T(8,128)(2,1)S(1)} %copy-done.7), kind=kOutput, calls=%fused_computation.37 | convolution fusion | flops 2044723200 | bytes 11272192 | tf_op jit(solution)/shard_map/dot_general | solution.py:134
  271.1 19.8 %collective-permute-done.7 = bf16[192,2560]{1,0:T(8,128)(2,1)} collective-permute-done((bf16[192,2560]{1,0:T(8,128)(2,1)}, bf16[192,2560]{1,0:T(8,128)(2,1)}, u32[]{:S(2)}, u32[]{:S(2)}) %collective-permute-start.7) | collective-permute-done | bytes 983072 | tf_op jit(solution)/shard_map/ppermute | solution.py:21
  291.0 32.6 %collective-permute-done.4 = bf16[256,384]{1,0:T(8,128)(2,1)S(1)} collective-permute-done((bf16[256,384]{1,0:T(8,128)(2,1)S(1)}, bf16[256,384]{1,0:T(8,128)(2,1)S(1)}, u32[]{:S(2)}, u32[]{:S(2)}) %collective-permute-start.4) | collective-permute-done | bytes 196640 | tf_op jit(solution)/shard_map/ppermute | solution.py:13
  323.6 4.4 convolution_convert_fusion.3
  328.0 4.6 %all-to-all-start.1 = ((bf16[16,16,2560]{2,1,0:T(8,128)(2,1)}), bf16[16,16,2560]{2,1,0:T(8,128)(2,1)}, u32[]{:S(2)}, u32[]{:S(2)}) async-start(bf16[16,16,2560]{2,1,0:T(8,128)(2,1)} %bitcast.178), calls=%async_computation.1 | async-start | bytes 2621440 | tf_op jit(solution)/shard_map/all_to_all | solution.py:148
  336.7 8.6 %fusion.10 = f32[256,768]{1,0:T(8,128)S(1)} fusion(bf16[256,5120]{1,0:T(8,128)(2,1)S(1)} %bitcast.173, bf16[192,5120]{1,0:T(8,128)(2,1)} %collective-permute-done.3, bf16[192,5120]{1,0:T(8,128)(2,1)S(1)} %copy-done.6, bf16[192,5120]{1,0:T(8,128)(2,1)} %collective-permute-done.2, bf16[192,5120]{1,0:T(8,128)(2,1)S(1)} %copy-done.8), kind=kOutput, calls=%fused_computation.36 | convolution fusion | flops 2044723200 | bytes 11272192 | tf_op jit(solution)/shard_map/dot_general | solution.py:134
  347.6 7.7 %collective-permute-done.18 = bf16[256,384]{1,0:T(8,128)(2,1)S(1)} collective-permute-done((bf16[256,384]{1,0:T(8,128)(2,1)S(1)}, bf16[256,384]{1,0:T(8,128)(2,1)S(1)}, u32[]{:S(2)}, u32[]{:S(2)}) %collective-permute-start.18) | collective-permute-done | bytes 196640 | tf_op jit(solution)/shard_map/ppermute | solution.py:13
  355.4 4.3 convolution_convert_fusion.1
  359.7 4.4 all-to-all-done.1
  364.1 4.4 all-to-all-start.5
  372.2 8.7 %fusion.8 = f32[256,768]{1,0:T(8,128)S(1)} fusion(bf16[256,5120]{1,0:T(8,128)(2,1)S(1)} %bitcast.174, bf16[192,5120]{1,0:T(8,128)(2,1)} %collective-permute-done.10, bf16[192,5120]{1,0:T(8,128)(2,1)S(1)} %copy-done.2, bf16[192,5120]{1,0:T(8,128)(2,1)} %collective-permute-done.9, bf16[192,5120]{1,0:T(8,128)(2,1)S(1)} %copy-done.4), kind=kOutput, calls=%fused_computation.34 | convolution fusion | flops 2044723200 | bytes 11272192 | tf_op jit(solution)/shard_map/dot_general | solution.py:134
  383.3 5.5 %collective-permute-done.20 = bf16[256,384]{1,0:T(8,128)(2,1)S(1)} collective-permute-done((bf16[256,384]{1,0:T(8,128)(2,1)S(1)}, bf16[256,384]{1,0:T(8,128)(2,1)S(1)}, u32[]{:S(2)}, u32[]{:S(2)}) %collective-permute-start.20) | collective-permute-done | bytes 196640 | tf_op jit(solution)/shard_map/ppermute | solution.py:13
  388.9 4.1 convolution_convert_fusion
  392.9 7.3 %all-to-all-done.5 = bf16[16,16,2560]{2,1,0:T(8,128)(2,1)} async-done(((bf16[16,16,2560]{2,1,0:T(8,128)(2,1)}), bf16[16,16,2560]{2,1,0:T(8,128)(2,1)}, u32[]{:S(2)}, u32[]{:S(2)}) %all-to-all-start.5) | async-done | bytes 1310752 | tf_op jit(solution)/shard_map/all_to_all | solution.py:148
  416.9 18.8 %all-to-all-done.7 = bf16[16,16,2560]{2,1,0:T(8,128)(2,1)S(1)} async-done(((bf16[16,16,2560]{2,1,0:T(8,128)(2,1)}), bf16[16,16,2560]{2,1,0:T(8,128)(2,1)S(1)}, u32[]{:S(2)}, u32[]{:S(2)}) %all-to-all-start.7) | async-done | bytes 1310752 | tf_op jit(solution)/shard_map/all_to_all | solution.py:148
  439.3 6.0 %collective-permute-done.21 = bf16[64,2560]{1,0:T(8,128)(2,1)S(1)} collective-permute-done((bf16[64,2560]{1,0:T(8,128)(2,1)S(1)}, bf16[64,2560]{1,0:T(8,128)(2,1)S(1)}, u32[]{:S(2)}, u32[]{:S(2)}) %collective-permute-start.21) | collective-permute-done | bytes 327712 | tf_op jit(solution)/shard_map/ppermute | solution.py:13
  (136 shorter events, 62.4 us)
Async XLA Ops:
  5.4 39.3 %all-to-all-start.2 = ((bf16[16,8,5120]{2,1,0:T(8,128)(2,1)}), bf16[16,8,5120]{2,1,0:T(8,128)(2,1)}, u32[]{:S(2)}, u32[]{:S(2)}) async-start(bf16[16,8,5120]{2,1,0:T(8,128)(2,1)} %fusion.74), calls=%async_computation.2 | async-start | bytes 2621440 | tf_op jit(solution)/shard_map/all_to_all | solution.py:131
  44.7 36.1 %all-to-all-start = ((bf16[16,8,5120]{2,1,0:T(8,128)(2,1)}), bf16[16,8,5120]{2,1,0:T(8,128)(2,1)}, u32[]{:S(2)}, u32[]{:S(2)}) async-start(bf16[16,8,5120]{2,1,0:T(8,128)(2,1)} %fusion.76), calls=%async_computation | async-start | bytes 2621440 | tf_op jit(solution)/shard_map/all_to_all | solution.py:131
  49.5 139.3 %copy-start.14 = (f32[64]{0:T(128)}, f32[64]{0:T(128)S(1)}, u32[]{:S(2)}) copy-start(f32[64]{0:T(128)S(1)} %add_rsqrt_fusion) | copy-start | bytes 772
  49.5 139.2 %copy-start.11 = (pred[64,2,1,8,8]{0,4,3,1,2:T(8,128)(4,1)}, pred[64,2,1,8,8]{0,4,3,1,2:T(8,128)(4,1)S(1)}, u32[]{:S(2)}) copy-start(pred[64,2,1,8,8]{0,4,3,1,2:T(8,128)(4,1)S(1)} %get-tuple-element.41) | copy-start | bytes 24580
  80.8 109.6 %all-to-all-start.6 = ((bf16[16,8,5120]{2,1,0:T(8,128)(2,1)}), bf16[16,8,5120]{2,1,0:T(8,128)(2,1)S(1)}, u32[]{:S(2)}, u32[]{:S(2)}) async-start(bf16[16,8,5120]{2,1,0:T(8,128)(2,1)} %fusion.78), calls=%async_computation.6 | async-start | bytes 2621440 | tf_op jit(solution)/shard_map/all_to_all | solution.py:131
  91.1 106.6 %collective-permute-start.10 = (bf16[192,5120]{1,0:T(8,128)(2,1)}, bf16[192,5120]{1,0:T(8,128)(2,1)}, u32[]{:S(2)}, u32[]{:S(2)}) collective-permute-start(bf16[192,5120]{1,0:T(8,128)(2,1)} %get-tuple-element.18), channel_id=1, source_target_pairs={{0,8},{8,0},{1,9},{9,1},{2,10},{10,2},{3,11},{11,3},{4,12},{12,4},... | collective-permute-start | bytes 5898248 | tf_op jit(solution)/shard_map/ppermute | solution.py:17
  98.1 99.8 %collective-permute-start.9 = (bf16[192,5120]{1,0:T(8,128)(2,1)}, bf16[192,5120]{1,0:T(8,128)(2,1)}, u32[]{:S(2)}, u32[]{:S(2)}) collective-permute-start(bf16[192,5120]{1,0:T(8,128)(2,1)} %get-tuple-element.14), channel_id=1, source_target_pairs={{0,8},{8,0},{1,9},{9,1},{2,10},{10,2},{3,11},{11,3},{4,12},{12,4},... | collective-permute-start | bytes 5898248 | tf_op jit(solution)/shard_map/ppermute | solution.py:17
  98.2 92.2 %collective-permute-start.8 = (bf16[16,8,5120]{2,1,0:T(8,128)(2,1)}, bf16[16,8,5120]{2,1,0:T(8,128)(2,1)}, u32[]{:S(2)}, u32[]{:S(2)}) collective-permute-start(bf16[16,8,5120]{2,1,0:T(8,128)(2,1)} %all-to-all-done.2), channel_id=1, source_target_pairs={{0,16},{16,0},{1,17},{17,1},{2,18},{18,2},{3,19},{19,3},{4,20},{20... | collective-permute-start | bytes 3932168 | tf_op jit(solution)/shard_map/ppermute | solution.py:13
  106.2 91.0 %collective-permute-start.12 = (bf16[192,2560]{1,0:T(8,128)(2,1)}, bf16[192,2560]{1,0:T(8,128)(2,1)}, u32[]{:S(2)}, u32[]{:S(2)}) collective-permute-start(bf16[192,2560]{1,0:T(8,128)(2,1)} %get-tuple-element.20), channel_id=1, source_target_pairs={{0,8},{8,0},{1,9},{9,1},{2,10},{10,2},{3,11},{11,3},{4,12},{12,4},... | collective-permute-start | bytes 2949128 | tf_op jit(solution)/shard_map/ppermute | solution.py:17
  106.3 101.9 %collective-permute-start.13 = (bf16[192,2560]{1,0:T(8,128)(2,1)}, bf16[192,2560]{1,0:T(8,128)(2,1)}, u32[]{:S(2)}, u32[]{:S(2)}) collective-permute-start(bf16[192,2560]{1,0:T(8,128)(2,1)} %get-tuple-element.26), channel_id=1, source_target_pairs={{0,16},{16,0},{1,17},{17,1},{2,18},{18,2},{3,19},{19,3},{4,20},{20... | collective-permute-start | bytes 2949128 | tf_op jit(solution)/shard_map/ppermute | solution.py:13
  190.4 24.4 %collective-permute-start.14 = (bf16[192,2560]{1,0:T(8,128)(2,1)}, bf16[192,2560]{1,0:T(8,128)(2,1)}, u32[]{:S(2)}, u32[]{:S(2)}) collective-permute-start(bf16[192,2560]{1,0:T(8,128)(2,1)} %get-tuple-element.25), channel_id=1, source_target_pairs={{0,24},{8,16},{16,8},{24,0},{1,25},{9,17},{17,9},{25,1},{2,26},{10... | collective-permute-start | bytes 2949128 | tf_op jit(solution)/shard_map/ppermute | solution.py:21
  190.4 61.4 %all-to-all-start.4 = ((bf16[16,8,5120]{2,1,0:T(8,128)(2,1)}), bf16[16,8,5120]{2,1,0:T(8,128)(2,1)}, u32[]{:S(2)}, u32[]{:S(2)}) async-start(bf16[16,8,5120]{2,1,0:T(8,128)(2,1)} %fusion.80), calls=%async_computation.4 | async-start | bytes 2621440 | tf_op jit(solution)/shard_map/all_to_all | solution.py:131
  197.2 61.2 %collective-permute-start.2 = (bf16[192,5120]{1,0:T(8,128)(2,1)}, bf16[192,5120]{1,0:T(8,128)(2,1)}, u32[]{:S(2)}, u32[]{:S(2)}) collective-permute-start(bf16[192,5120]{1,0:T(8,128)(2,1)} %get-tuple-element.12), channel_id=1, source_target_pairs={{0,8},{8,0},{1,9},{9,1},{2,10},{10,2},{3,11},{11,3},{4,12},{12,4},... | collective-permute-start | bytes 5898248 | tf_op jit(solution)/shard_map/ppermute | solution.py:17
  197.7 62.1 %collective-permute-start.3 = (bf16[192,5120]{1,0:T(8,128)(2,1)}, bf16[192,5120]{1,0:T(8,128)(2,1)}, u32[]{:S(2)}, u32[]{:S(2)}) collective-permute-start(bf16[192,5120]{1,0:T(8,128)(2,1)} %get-tuple-element.16), channel_id=1, source_target_pairs={{0,8},{8,0},{1,9},{9,1},{2,10},{10,2},{3,11},{11,3},{4,12},{12,4},... | collective-permute-start | bytes 5898248 | tf_op jit(solution)/shard_map/ppermute | solution.py:17
  197.8 53.9 %collective-permute-start.1 = (bf16[16,8,5120]{2,1,0:T(8,128)(2,1)}, bf16[16,8,5120]{2,1,0:T(8,128)(2,1)}, u32[]{:S(2)}, u32[]{:S(2)}) collective-permute-start(bf16[16,8,5120]{2,1,0:T(8,128)(2,1)} %all-to-all-done), channel_id=1, source_target_pairs={{0,16},{16,0},{1,17},{17,1},{2,18},{18,2},{3,19},{19,3},{4,20},{20... | collective-permute-start | bytes 3932168 | tf_op jit(solution)/shard_map/ppermute | solution.py:13
  208.2 36.9 %collective-permute-start.11 = (bf16[256,384]{1,0:T(8,128)(2,1)S(1)}, bf16[256,384]{1,0:T(8,128)(2,1)S(1)}, u32[]{:S(2)}, u32[]{:S(2)}) collective-permute-start(bf16[256,384]{1,0:T(8,128)(2,1)S(1)} %bitcast.186), channel_id=1, source_target_pairs={{0,16},{16,0},{1,17},{17,1},{2,18},{18,2},{3,19},{19,3},{4,20},{20... | collective-permute-start | bytes 589832 | tf_op jit(solution)/shard_map/ppermute | solution.py:13
  214.7 55.8 %collective-permute-start.5 = (bf16[192,2560]{1,0:T(8,128)(2,1)}, bf16[192,2560]{1,0:T(8,128)(2,1)}, u32[]{:S(2)}, u32[]{:S(2)}) collective-permute-start(bf16[192,2560]{1,0:T(8,128)(2,1)} %get-tuple-element.23), channel_id=1, source_target_pairs={{0,8},{8,0},{1,9},{9,1},{2,10},{10,2},{3,11},{11,3},{4,12},{12,4},... | collective-permute-start | bytes 2949128 | tf_op jit(solution)/shard_map/ppermute | solution.py:17
  245.1 26.1 %collective-permute-start.6 = (bf16[192,2560]{1,0:T(8,128)(2,1)}, bf16[192,2560]{1,0:T(8,128)(2,1)}, u32[]{:S(2)}, u32[]{:S(2)}) collective-permute-start(bf16[192,2560]{1,0:T(8,128)(2,1)} %get-tuple-element.22), channel_id=1, source_target_pairs={{0,16},{16,0},{1,17},{17,1},{2,18},{18,2},{3,19},{19,3},{4,20},{20... | collective-permute-start | bytes 2949128 | tf_op jit(solution)/shard_map/ppermute | solution.py:13
  251.8 39.2 %collective-permute-start.7 = (bf16[192,2560]{1,0:T(8,128)(2,1)}, bf16[192,2560]{1,0:T(8,128)(2,1)}, u32[]{:S(2)}, u32[]{:S(2)}) collective-permute-start(bf16[192,2560]{1,0:T(8,128)(2,1)} %get-tuple-element.21), channel_id=1, source_target_pairs={{0,24},{8,16},{16,8},{24,0},{1,25},{9,17},{17,9},{25,1},{2,26},{10... | collective-permute-start | bytes 2949128 | tf_op jit(solution)/shard_map/ppermute | solution.py:21
  251.8 76.2 %all-to-all-start.3 = ((bf16[16,16,2560]{2,1,0:T(8,128)(2,1)}), bf16[16,16,2560]{2,1,0:T(8,128)(2,1)}, u32[]{:S(2)}, u32[]{:S(2)}) async-start(bf16[16,16,2560]{2,1,0:T(8,128)(2,1)} %bitcast.176), calls=%async_computation.3 | async-start | bytes 2621440 | tf_op jit(solution)/shard_map/all_to_all | solution.py:148
  258.4 74.2 %collective-permute-start.17 = (bf16[16,8,5120]{2,1,0:T(8,128)(2,1)}, bf16[16,8,5120]{2,1,0:T(8,128)(2,1)}, u32[]{:S(2)}, u32[]{:S(2)}) collective-permute-start(bf16[16,8,5120]{2,1,0:T(8,128)(2,1)} %all-to-all-done.4), channel_id=1, source_target_pairs={{0,16},{16,0},{1,17},{17,1},{2,18},{18,2},{3,19},{19,3},{4,20},{20... | collective-permute-start | bytes 3932168 | tf_op jit(solution)/shard_map/ppermute | solution.py:13
  269.0 54.5 %collective-permute-start.4 = (bf16[256,384]{1,0:T(8,128)(2,1)S(1)}, bf16[256,384]{1,0:T(8,128)(2,1)S(1)}, u32[]{:S(2)}, u32[]{:S(2)}) collective-permute-start(bf16[256,384]{1,0:T(8,128)(2,1)S(1)} %bitcast.185), channel_id=1, source_target_pairs={{0,16},{16,0},{1,17},{17,1},{2,18},{18,2},{3,19},{19,3},{4,20},{20... | collective-permute-start | bytes 589832 | tf_op jit(solution)/shard_map/ppermute | solution.py:13
  270.5 98.0 %collective-permute-start.19 = (bf16[16,8,5120]{2,1,0:T(8,128)(2,1)S(1)}, bf16[16,8,5120]{2,1,0:T(8,128)(2,1)}, u32[]{:S(2)}, u32[]{:S(2)}) collective-permute-start(bf16[16,8,5120]{2,1,0:T(8,128)(2,1)S(1)} %all-to-all-done.6), channel_id=1, source_target_pairs={{0,16},{16,0},{1,17},{17,1},{2,18},{18,2},{3,19},{19,3},{4,20},{20... | collective-permute-start | bytes 3932168 | tf_op jit(solution)/shard_map/ppermute | solution.py:13
  328.0 36.1 %all-to-all-start.1 = ((bf16[16,16,2560]{2,1,0:T(8,128)(2,1)}), bf16[16,16,2560]{2,1,0:T(8,128)(2,1)}, u32[]{:S(2)}, u32[]{:S(2)}) async-start(bf16[16,16,2560]{2,1,0:T(8,128)(2,1)} %bitcast.178), calls=%async_computation.1 | async-start | bytes 2621440 | tf_op jit(solution)/shard_map/all_to_all | solution.py:148
  345.5 9.9 %collective-permute-start.18 = (bf16[256,384]{1,0:T(8,128)(2,1)S(1)}, bf16[256,384]{1,0:T(8,128)(2,1)S(1)}, u32[]{:S(2)}, u32[]{:S(2)}) collective-permute-start(bf16[256,384]{1,0:T(8,128)(2,1)S(1)} %bitcast.188), channel_id=1, source_target_pairs={{0,16},{16,0},{1,17},{17,1},{2,18},{18,2},{3,19},{19,3},{4,20},{20... | collective-permute-start | bytes 589832 | tf_op jit(solution)/shard_map/ppermute | solution.py:13
  364.1 36.1 %all-to-all-start.5 = ((bf16[16,16,2560]{2,1,0:T(8,128)(2,1)}), bf16[16,16,2560]{2,1,0:T(8,128)(2,1)}, u32[]{:S(2)}, u32[]{:S(2)}) async-start(bf16[16,16,2560]{2,1,0:T(8,128)(2,1)} %bitcast.177), calls=%async_computation.5 | async-start | bytes 2621440 | tf_op jit(solution)/shard_map/all_to_all | solution.py:148
  381.1 7.8 %collective-permute-start.20 = (bf16[256,384]{1,0:T(8,128)(2,1)S(1)}, bf16[256,384]{1,0:T(8,128)(2,1)S(1)}, u32[]{:S(2)}, u32[]{:S(2)}) collective-permute-start(bf16[256,384]{1,0:T(8,128)(2,1)S(1)} %bitcast.187), channel_id=1, source_target_pairs={{0,16},{16,0},{1,17},{17,1},{2,18},{18,2},{3,19},{19,3},{4,20},{20... | collective-permute-start | bytes 589832 | tf_op jit(solution)/shard_map/ppermute | solution.py:13
  383.2 23.3 %collective-permute-start.16 = (bf16[2,64,16,8]{1,3,2,0:T(8,128)(2,1)S(1)}, bf16[2,64,16,8]{1,3,2,0:T(8,128)(2,1)S(1)}, u32[]{:S(2)}, u32[]{:S(2)}) collective-permute-start(bf16[2,64,16,8]{1,3,2,0:T(8,128)(2,1)S(1)} %get-tuple-element.38), channel_id=1, source_target_pairs={{0,16},{16,0},{1,17},{17,1},{2,18},{18,2},{3,19},{19,3},{4,20},{20... | collective-permute-start | bytes 98312 | tf_op jit(solution)/shard_map/ppermute | solution.py:13
  400.2 35.5 %all-to-all-start.7 = ((bf16[16,16,2560]{2,1,0:T(8,128)(2,1)}), bf16[16,16,2560]{2,1,0:T(8,128)(2,1)S(1)}, u32[]{:S(2)}, u32[]{:S(2)}) async-start(bf16[16,16,2560]{2,1,0:T(8,128)(2,1)} %bitcast.83), calls=%async_computation.7 | async-start | bytes 2621440 | tf_op jit(solution)/shard_map/all_to_all | solution.py:148
  404.4 4.8 %collective-permute-start = (bf16[2,64,16,8]{1,3,2,0:T(8,128)(2,1)S(1)}, bf16[2,64,16,8]{1,3,2,0:T(8,128)(2,1)S(1)}, u32[]{:S(2)}, u32[]{:S(2)}) collective-permute-start(bf16[2,64,16,8]{1,3,2,0:T(8,128)(2,1)S(1)} %get-tuple-element.36), channel_id=1, source_target_pairs={{0,16},{16,0},{1,17},{17,1},{2,18},{18,2},{3,19},{19,3},{4,20},{20... | collective-permute-start | bytes 98312 | tf_op jit(solution)/shard_map/ppermute | solution.py:13
  413.4 24.8 %collective-permute-start.15 = (bf16[64,2560]{1,0:T(8,128)(2,1)}, bf16[64,2560]{1,0:T(8,128)(2,1)}, u32[]{:S(2)}, u32[]{:S(2)}) collective-permute-start(bf16[64,2560]{1,0:T(8,128)(2,1)} %slice.91), channel_id=1, source_target_pairs={{0,16},{16,0},{1,17},{17,1},{2,18},{18,2},{3,19},{19,3},{4,20},{20... | collective-permute-start | bytes 983048 | tf_op jit(solution)/shard_map/ppermute | solution.py:13
  436.1 9.2 %collective-permute-start.21 = (bf16[64,2560]{1,0:T(8,128)(2,1)S(1)}, bf16[64,2560]{1,0:T(8,128)(2,1)S(1)}, u32[]{:S(2)}, u32[]{:S(2)}) collective-permute-start(bf16[64,2560]{1,0:T(8,128)(2,1)S(1)} %slice.99), channel_id=1, source_target_pairs={{0,16},{16,0},{1,17},{17,1},{2,18},{18,2},{3,19},{19,3},{4,20},{20... | collective-permute-start | bytes 983048 | tf_op jit(solution)/shard_map/ppermute | solution.py:13
  (14 other events, 73.0 us)

commit v2 on v1

v2 whole, which is shorter than its diff:
```python
import jax
import jax.numpy as jnp
from jax import lax
from jax.sharding import Mesh, PartitionSpec as P

epsilon = 1e-05
contract = (((1,), (1,)), ((), ()))
swap = [(0, 1), (1, 0)]
group = ("core", "inner")


def side_swap(values):
    return lax.ppermute(values, "side", swap)


def core_swap(values):
    return lax.ppermute(values, "core", swap)


def far_swap(values):
    return lax.ppermute(values, "far", swap)


def cross_swap(values):
    return lax.ppermute(values, ("side", "core"), [(0, 3), (1, 2), (2, 1), (3, 0)])


def normalise(rows, norm_gain):
    current = rows.astype(jnp.float32)
    inverse_rms = lax.rsqrt(jnp.mean(current * current, axis=-1, keepdims=True) + epsilon)
    return (current * inverse_rms * norm_gain).astype(jnp.bfloat16)


def all_router_rows(router_weight):
    axes = ("side", "core", "far", "inner")
    row = router_weight.reshape(1, -1)
    copies = jnp.broadcast_to(row, (lax.axis_size(axes), row.shape[1]))
    return lax.all_to_all(copies, axes, split_axis=0, concat_axis=0, tiled=True)


def on_device(activations, norm_gain, router_weight, gate_proj, up_proj, down_proj, expert_ids):
    steps, rows, width = activations.shape
    top = expert_ids.shape[2]
    cores, fars, inners = (lax.axis_size(name) for name in ("core", "far", "inner"))
    local = gate_proj.shape[0] // cores
    experts = gate_proj.shape[0] * fars * inners
    capacity = max(2, 2 * top * rows // experts)
    part = gate_proj.shape[2]
    half = width // 2
    side, core, far = (lax.axis_index(name) for name in ("side", "core", "far"))
    peers = cores * inners
    slots = local * capacity

    raw = [[activations[step], far_swap(activations[step])] for step in range(steps)]
    crossed = [step % 2 == 1 for step in range(steps)]
    raw_other = [
        [side_swap(raw[step][kind]) for kind in range(2)] if crossed[step] else None
        for step in range(steps)
    ]

    ids = jnp.stack([expert_ids, side_swap(expert_ids)])
    ids = jnp.stack([ids, far_swap(ids)])
    named = jnp.any(ids[..., None] == jnp.arange(experts, dtype=jnp.int32), axis=4)
    lower = jnp.tril(jnp.ones((rows, rows), jnp.bfloat16), -1)
    earlier = jnp.einsum(
        "rq,kpsqe->kpsre", lower, named.astype(jnp.bfloat16), preferred_element_type=jnp.float32
    )
    near_half = (2, 2, steps, rows, cores, local, fars, inners)
    mine = lax.dynamic_index_in_dim(named.reshape(near_half), far, 6, keepdims=False)
    rank = lax.dynamic_index_in_dim(earlier.reshape(near_half), far, 6, keepdims=False)
    taken = mine[..., None] & (rank[..., None] == jnp.arange(capacity, dtype=jnp.float32))
    taken = jnp.moveaxis(taken, 5, 6).astype(jnp.bfloat16)

    def expert_block(weights, which_core):
        return lax.dynamic_slice_in_dim(weights, which_core * local, local, 0)[:, 0]

    def down_block(which_core, which_side):
        return lax.dynamic_slice(
            down_proj,
            (which_core * local, 0, 0, which_side * half),
            (local, 1, part, half),
        )[:, 0]

    down_side = side_swap(down_block(core, 1 - side))
    down_cross = cross_swap(down_block(1 - core, 1 - side))
    gate_up = jnp.concatenate(
        [
            expert_block(gate_proj, core),
            core_swap(expert_block(gate_proj, 1 - core)),
            expert_block(up_proj, core),
            core_swap(expert_block(up_proj, 1 - core)),
        ],
        axis=1,
    )
    down = jnp.concatenate(
        [
            down_block(core, side),
            core_swap(down_block(1 - core, side)),
            down_side,
            down_cross,
        ],
        axis=1,
    )
    gate_up, down = lax.optimization_barrier((gate_up, down))

    router_rows = all_router_rows(router_weight)
    normed = [normalise(activations[step], norm_gain) for step in range(steps)]
    own_named = named[0, 0]
    scores = []
    for step in range(steps):
        logits = lax.dot_general(
            normed[step], router_rows, contract, preferred_element_type=jnp.float32
        )
        scores.append(
            jnp.where(own_named[step], jax.nn.sigmoid(logits).astype(jnp.bfloat16), 0)
        )
    scores = jnp.stack(scores)
    scores = jnp.stack([scores, side_swap(scores)])
    total = jnp.sum(scores.astype(jnp.float32), axis=3, keepdims=True)
    scores = jnp.stack([scores, far_swap(scores)])
    near_scores = lax.dynamic_index_in_dim(scores.reshape(near_half), far, 6, keepdims=False)
    weighted = taken * jnp.moveaxis(near_scores, 5, 6)[..., None]
    planes = jnp.eye(2, dtype=jnp.bfloat16)
    scatter = jnp.einsum("kpsrcnlt,pq->ksprcnqlt", weighted, planes).reshape(
        2, steps, 2 * rows, peers * 2 * slots
    )

    def forward(step, kind):
        if crossed[step]:
            source = jnp.concatenate([raw[step][kind], raw_other[step][kind]], axis=0)
            pack = jnp.einsum("prcnlt,pq->cnqltpr", taken[kind, :, step], planes)
            pack = pack.reshape(peers * 2 * slots, 2 * rows)
            outgoing = jnp.dot(pack, normalise(source, norm_gain)).reshape(
                peers, 2 * slots, width
            )
            both = lax.all_to_all(outgoing, group, split_axis=0, concat_axis=0, tiled=True)
            both = both.reshape(peers, 2, local, capacity, width)
        else:
            pack = jnp.einsum("rcnlt->cnltr", taken[kind, 0, step]).reshape(peers * slots, rows)
            outgoing = jnp.dot(pack, normalise(raw[step][kind], norm_gain)).reshape(
                peers, slots, width
            )
            near = lax.all_to_all(outgoing, group, split_axis=0, concat_axis=0, tiled=True)
            other = side_swap(near)
            both = jnp.stack([near, other], axis=1).reshape(peers, 2, local, capacity, width)
        return both

    def apply(both):
        inputs = jnp.moveaxis(both, 2, 0).reshape(local, -1, width)
        products = jnp.einsum("ird,iud->iru", inputs, gate_up, preferred_element_type=jnp.float32)
        gate_part, up_part = jnp.split(products, 2, axis=2)
        hidden = (jax.nn.silu(gate_part) * up_part).astype(jnp.bfloat16)
        units = hidden.shape[2]
        flipped = jnp.flip(hidden.reshape(local, peers, 2, capacity, units), axis=2)
        other_hidden = side_swap(flipped.reshape(hidden.shape))
        result = jnp.einsum(
            "iru,iud->ird",
            jnp.concatenate([hidden, other_hidden], axis=2),
            down,
            preferred_element_type=jnp.float32,
        ).astype(jnp.bfloat16)
        result = jnp.moveaxis(result.reshape(local, peers, 2, capacity, half), 0, 2)
        returned = lax.all_to_all(
            result.reshape(peers, 2 * slots, half),
            group,
            split_axis=0,
            concat_axis=0,
            tiled=True,
        )
        return returned.reshape(-1, half)

    outputs = []
    for step in range(steps):
        sums = [
            jnp.dot(
                scatter[kind, step],
                apply(forward(step, kind)),
                preferred_element_type=jnp.float32,
            )
            for kind in (0, 1)
        ]
        from_far = far_swap(sums[1].astype(jnp.bfloat16)).astype(jnp.float32)
        mixture = (sums[0] + from_far) / total[:, step].reshape(2 * rows, 1)
        mixture = mixture.astype(jnp.bfloat16)
        own, received = mixture[:rows], side_swap(mixture[rows:])
        low = jnp.where(side == 0, own, received)
        high = jnp.where(side == 0, received, own)
        outputs.append(jnp.concatenate([low, high], axis=1))
    return jnp.stack(outputs)


def solution(mesh):
    sections, columns = mesh.shape["section"], mesh.shape["expert"]
    split = Mesh(
        mesh.devices.reshape(2, sections // 2, 2, columns // 2),
        ("side", "core", "far", "inner"),
    )
    everywhere = ("side", "core", "far", "inner")
    weights = P(None, ("far", "inner"), ("side", "core"), None)
    return jax.shard_map(
        on_device,
        mesh=split,
        in_specs=(
            P(None, everywhere, None),
            P(),
            P(None, everywhere),
            weights,
            weights,
            weights,
            P(None, everywhere, None),
        ),
        out_specs=P(None, everywhere, None),
        check_vma=False,
    )
```

time: 448 us -> 482 us (1.076); the launches traced: 447 us -> 472 us
  blocking collectives: 73.2 us -> 0 us
  waiting for transfers between devices: 200 us -> 251 us
  matrix products: 65.2 us -> 79.8 us
  local copies, waits for them, and re-layouts: 28.1 us -> 41.6 us
  other arithmetic: 20.1 us -> 30.9 us
  starting transfers between devices: 58.9 us -> 68.2 us
    ppermute x0 -> x6, waiting for transfers between devices: none -> 134 us  [far_swap(): return lax.ppermute(values, 'far', swap)]
    all_to_all x8 -> x9, waiting for transfers between devices: 90.3 us -> 0.02 us  [the longest x4 0.01 us: forward(): lax.all_to_all(outgoing, group, split_axis=0, concat_axis=0, tiled=True)]
    all_gather x1 -> x0, blocking collectives: 73.2 us -> none  [on_device(): lax.all_gather(router_weight.reshape(1, width), ('side', 'core', 'expert'...]
    ppermute x14 -> x13, waiting for transfers between devices: 84.6 us -> 117 us  [side_swap(): return lax.ppermute(values, 'side', swap)]
    ppermute x2 -> x1, waiting for transfers between devices: 25.4 us -> 0.01 us  [cross_swap(): lax.ppermute(values, ('side', 'core'), [(0, 3), (1, 2), (2, 1), (3, 0)])]
    concatenate x0 -> x2, other arithmetic: none -> 16.8 us  [the longest x1 9.99 us: on_device(): jnp.concatenate([expert_block(gate_proj, core), core_swap(expert_block(ga...]
    dot_general x16 -> x17, matrix products: 64.4 us -> 76.9 us  [the longest x4 42.9 us: apply(): jnp.einsum('ird,iud->iru', inputs, gate_up, preferred_element_type=jnp.fl...]
    ppermute x0 -> x6, starting transfers between devices: none -> 7.67 us  [far_swap(): return lax.ppermute(values, 'far', swap)]
  transfers between devices with their start and end apart: 30 -> 32, of which waited for: 13 -> 16; matrix products, arithmetic and copies ran while one was open for 23% -> 31% of each run, Pallas kernels for 0% -> 0%
where the time goes in v2:
time: 482 us; the launch traced here: 472 us
  waiting for transfers between devices  251 us (52%)
  matrix products  79.8 us (17%)
  starting transfers between devices  68.2 us (14%)
  local copies, waits for them, and re-layouts  41.6 us (9%)
  other arithmetic  30.9 us (6%)
    ppermute x6, waiting for transfers between devices, far_swap(): return lax.ppermute(values, 'far', swap)  134 us
    ppermute x13, waiting for transfers between devices, side_swap(): return lax.ppermute(values, 'side', swap)  117 us
    dot_general x4, matrix products, apply(): jnp.einsum('ird,iud->iru', inputs, gate_up, preferred_element_type=jnp.fl...  42.9 us
    all_to_all x4, starting transfers between devices, apply(): lax.all_to_all(result.reshape(peers, 2 * slots, half), group, split_axis=...  19.3 us
    ppermute x13, starting transfers between devices, side_swap(): return lax.ppermute(values, 'side', swap)  18.5 us
    dot_general x4, matrix products, apply(): jnp.einsum('iru,iud->ird', jnp.concatenate([hidden, other_hidden], axis=2...  17.7 us
    all_to_all x4, starting transfers between devices, forward(): lax.all_to_all(outgoing, group, split_axis=0, concat_axis=0, tiled=True)  16.3 us
    squeeze x2, local copies, waits for them, and re-layouts, expert_block(): return lax.dynamic_slice_in_dim(weights, which_core * local, local, 0)[:, 0]  13.8 us
  transfers between devices with their start and end apart: 32, of which 16 were waited for; matrix products, arithmetic and copies ran while one was open for 31% of the time, Pallas kernels for 0%

profile of v2, /device:TPU:0, one launch (start us, length us, event | category | flops | bytes accessed | tf_op | source)
XLA Modules:
  0.0 472.5 jit_solution(11596180222149471284)
XLA Ops:
  8.2 4.9 %all-to-all-start = ((bf16[32,2,2560]{2,1,0:T(2,128)(2,1)}), bf16[32,2,2560]{2,1,0:T(2,128)(2,1)S(1)}, u32[]{:S(2)}, u32[]{:S(2)}) async-start(bf16[32,2,2560]{2,1,0:T(2,128)(2,1)} %reshape.287), calls=%async_computation | async-start | bytes 655360 | tf_op jit(solution)/shard_map/all_to_all | solution.py:38
  16.3 7.8 %collective-permute-done.1 = s32[2,2,64,2]{2,3,1,0:T(2,128)S(1)} collective-permute-done((s32[2,2,64,2]{2,3,1,0:T(2,128)S(1)}, s32[2,2,64,2]{2,3,1,0:T(2,128)S(1)}, u32[]{:S(2)}, u32[]{:S(2)}) %collective-permute-start.1) | collective-permute-done | bytes 2080 | tf_op jit(solution)/shard_map/ppermute | solution.py:21
  31.4 31.4 %collective-permute-done.11 = bf16[64,5120]{1,0:T(8,128)(2,1)S(1)} collective-permute-done((bf16[64,5120]{1,0:T(8,128)(2,1)S(1)}, bf16[64,5120]{1,0:T(8,128)(2,1)S(1)}, u32[]{:S(2)}, u32[]{:S(2)}) %collective-permute-start.11) | collective-permute-done | bytes 655392 | tf_op jit(solution)/shard_map/ppermute | solution.py:21
  64.8 4.3 all-to-all-start.3
  71.1 14.9 %collective-permute-done.16 = bf16[64,5120]{1,0:T(8,128)(2,1)S(1)} collective-permute-done((bf16[64,5120]{1,0:T(8,128)(2,1)S(1)}, bf16[64,5120]{1,0:T(8,128)(2,1)S(1)}, u32[]{:S(2)}, u32[]{:S(2)}) %collective-permute-start.16) | collective-permute-done | bytes 655392 | tf_op jit(solution)/shard_map/ppermute | solution.py:13
  93.1 6.9 %dynamic-slice_bitcast_fusion.1 = (bf16[2,192,5120]{2,1,0:T(8,128)(2,1)}, bf16[2,192,5120]{2,1,0:T(8,128)(2,1)}) fusion(bf16[4,1,192,5120]{3,2,1,0:T(8,128)(2,1)} %param.11, s32[]{:T(128)S(6)} %select_n.64, s32[]{:T(128)S(6)} %select_n.65), kind=kLoop, calls=%fused_computation.3 | loop fusion | bytes 15728648 | tf_op jit(solution)/shard_map/squeeze | solution.py:75
  100.2 6.6 %dynamic-slice_bitcast_fusion.7 = (bf16[2,192,2560]{2,1,0:T(8,128)(2,1)}, bf16[2,192,2560]{2,1,0:T(8,128)(2,1)}, bf16[2,192,2560]{2,1,0:T(8,128)(2,1)}, bf16[2,192,2560]{2,1,0:T(8,128)(2,1)}) fusion(bf16[4,1,192,5120]{3,2,1,0:T(8,128)(2,1)} %param.12, s32[]{:T(128)S(6)} %select_n.64, s32[]{:T(128)S(6)} %select_n.66, s32[]{:T(128)S(6)} %select_n.65, ...), kind=kLoop, calls=%fused_computation.27 | loop fusion | bytes 15728656 | tf_op jit(solution)/shard_map/squeeze | solution.py:78
  108.2 27.8 %collective-permute-done.18 = bf16[64,5120]{1,0:T(8,128)(2,1)} collective-permute-done((bf16[64,5120]{1,0:T(8,128)(2,1)S(1)}, bf16[64,5120]{1,0:T(8,128)(2,1)}, u32[]{:S(2)}, u32[]{:S(2)}) %collective-permute-start.18) | collective-permute-done | bytes 655392 | tf_op jit(solution)/shard_map/ppermute | solution.py:21
  137.4 6.9 %dynamic-slice_bitcast_fusion.3 = (bf16[2,192,5120]{2,1,0:T(8,128)(2,1)}, bf16[2,192,5120]{2,1,0:T(8,128)(2,1)}) fusion(bf16[4,1,192,5120]{3,2,1,0:T(8,128)(2,1)} %param.10, s32[]{:T(128)S(6)} %select_n.64, s32[]{:T(128)S(6)} %select_n.65), kind=kLoop, calls=%fused_computation.5 | loop fusion | bytes 15728648 | tf_op jit(solution)/shard_map/squeeze | solution.py:75
  144.9 21.7 %collective-permute-done.19 = bf16[64,5120]{1,0:T(8,128)(2,1)S(1)} collective-permute-done((bf16[64,5120]{1,0:T(8,128)(2,1)}, bf16[64,5120]{1,0:T(8,128)(2,1)S(1)}, u32[]{:S(2)}, u32[]{:S(2)}) %collective-permute-start.19) | collective-permute-done | bytes 655392 | tf_op jit(solution)/shard_map/ppermute | solution.py:13
  175.3 4.6 all-to-all-start.7
  179.9 29.0 %collective-permute-done.8 = bf16[2,192,2560]{2,1,0:T(8,128)(2,1)} collective-permute-done((bf16[2,192,2560]{2,1,0:T(8,128)(2,1)}, bf16[2,192,2560]{2,1,0:T(8,128)(2,1)}, u32[]{:S(2)}, u32[]{:S(2)}) %collective-permute-start.8) | collective-permute-done | bytes 1966112 | tf_op jit(solution)/shard_map/ppermute | solution.py:13
  208.8 6.8 %pad_maximum_fusion.1 = bf16[2,768,2560]{2,1,0:T(8,128)(2,1)} fusion(bf16[2,192,2560]{2,1,0:T(8,128)(2,1)} %collective-permute-done.9, bf16[2,192,2560]{2,1,0:T(8,128)(2,1)} %collective-permute-done.8, bf16[2,192,2560]{2,1,0:T(8,128)(2,1)} %collective-permute-done.7, bf16[2,192,2560]{2,1,0:T(8,128)(2,1)} %get-tuple-element.13), kind=kLoop, calls=%fused_computation.1 | loop fusion | flops 31457280 | bytes 15728640 | tf_op jit(solution)/shard_map/concatenate | solution.py:95
  217.1 19.8 %collective-permute-done.4 = bf16[8,16,5120]{2,1,0:T(8,128)(2,1)} collective-permute-done((bf16[8,16,5120]{2,1,0:T(8,128)(2,1)}, bf16[8,16,5120]{2,1,0:T(8,128)(2,1)}, u32[]{:S(2)}, u32[]{:S(2)}) %collective-permute-start.4) | collective-permute-done | bytes 1310752 | tf_op jit(solution)/shard_map/ppermute | solution.py:13
  240.9 10.0 %pad_maximum_fusion = bf16[2,768,5120]{2,1,0:T(8,128)(2,1)} fusion(bf16[2,192,5120]{2,1,0:T(8,128)(2,1)} %collective-permute-done.6, bf16[2,192,5120]{2,1,0:T(8,128)(2,1)S(1)} %copy-done, bf16[2,192,5120]{2,1,0:T(8,128)(2,1)} %collective-permute-done.5, bf16[2,192,5120]{2,1,0:T(8,128)(2,1)S(1)} %copy-done.1), kind=kLoop, calls=%fused_computation | loop fusion | flops 62914560 | bytes 31457280 | tf_op jit(solution)/shard_map/concatenate | solution.py:86
  250.9 10.7 %fusion.90 = f32[2,128,768]{2,1,0:T(8,128)S(1)} fusion(bf16[2,128,5120]{2,1,0:T(8,128)(2,1)S(1)} %bitcast.202, bf16[2,768,5120]{2,1,0:T(8,128)(2,1)} %pad_maximum_fusion), kind=kOutput, calls=%fused_computation.167 | convolution fusion | flops 2013265920 | bytes 19136512 | tf_op jit(solution)/shard_map/ird,iud->iru/dot_general | solution.py:150
  263.4 5.4 %collective-permute-done.10 = bf16[2,128,384]{2,1,0:T(8,128)(2,1)S(1)} collective-permute-done((bf16[2,128,384]{2,1,0:T(8,128)(2,1)S(1)}, bf16[2,128,384]{2,1,0:T(8,128)(2,1)S(1)}, u32[]{:S(2)}, u32[]{:S(2)}) %collective-permute-start.10) | collective-permute-done | bytes 196640 | tf_op jit(solution)/shard_map/ppermute | solution.py:13
  268.7 4.4 convolution_convert_fusion.3
  280.8 10.7 %fusion.91 = f32[2,128,768]{2,1,0:T(8,128)S(1)} fusion(bf16[2,128,5120]{2,1,0:T(8,128)(2,1)S(1)} %bitcast.204, bf16[2,768,5120]{2,1,0:T(8,128)(2,1)} %pad_maximum_fusion), kind=kOutput, calls=%fused_computation.168 | convolution fusion | flops 2013265920 | bytes 19136512 | tf_op jit(solution)/shard_map/ird,iud->iru/dot_general | solution.py:150
  299.0 4.4 convolution_convert_fusion.2
  304.6 4.5 all-to-all-start.4
  312.2 10.7 %fusion.93 = f32[2,128,768]{2,1,0:T(8,128)S(1)} fusion(bf16[2,128,5120]{2,1,0:T(8,128)(2,1)S(1)} %bitcast.205, bf16[2,768,5120]{2,1,0:T(8,128)(2,1)} %pad_maximum_fusion), kind=kOutput, calls=%fused_computation.170 | convolution fusion | flops 2013265920 | bytes 19136512 | tf_op jit(solution)/shard_map/ird,iud->iru/dot_general | solution.py:150
  330.7 4.4 convolution_convert_fusion
  336.3 4.3 all-to-all-start.8
  343.2 13.1 %collective-permute-done.3 = bf16[2,2,64,32]{2,3,1,0:T(8,128)(2,1)S(1)} collective-permute-done((bf16[2,2,64,32]{2,3,1,0:T(8,128)(2,1)S(1)}, bf16[2,2,64,32]{2,3,1,0:T(8,128)(2,1)S(1)}, u32[]{:S(2)}, u32[]{:S(2)}) %collective-permute-start.3) | collective-permute-done | bytes 16416 | tf_op jit(solution)/shard_map/ppermute | solution.py:21
  359.0 10.7 %fusion.92 = f32[2,128,768]{2,1,0:T(8,128)S(1)} fusion(bf16[2,128,5120]{2,1,0:T(8,128)(2,1)S(1)} %bitcast.203, bf16[2,768,5120]{2,1,0:T(8,128)(2,1)} %pad_maximum_fusion), kind=kOutput, calls=%fused_computation.169 | convolution fusion | flops 2013265920 | bytes 19136512 | tf_op jit(solution)/shard_map/ird,iud->iru/dot_general | solution.py:150
  376.6 4.4 convolution_convert_fusion.1
  382.3 6.2 %all-to-all-start.6 = ((bf16[8,32,2560]{2,1,0:T(8,128)(2,1)}), bf16[8,32,2560]{2,1,0:T(8,128)(2,1)S(1)}, u32[]{:S(2)}, u32[]{:S(2)}) async-start(bf16[8,32,2560]{2,1,0:T(8,128)(2,1)} %bitcast.82), calls=%async_computation.6 | async-start | bytes 2621440 | tf_op jit(solution)/shard_map/all_to_all | solution.py:163
  392.3 30.9 %collective-permute-done.14 = bf16[128,2560]{1,0:T(8,128)(2,1)S(1)} collective-permute-done((bf16[128,2560]{1,0:T(8,128)(2,1)S(1)}, bf16[128,2560]{1,0:T(8,128)(2,1)S(1)}, u32[]{:S(2)}, u32[]{:S(2)}) %collective-permute-start.14) | collective-permute-done | bytes 655392 | tf_op jit(solution)/shard_map/ppermute | solution.py:21
  429.4 6.1 %collective-permute-done.15 = bf16[64,2560]{1,0:T(8,128)(2,1)} collective-permute-done((bf16[64,2560]{1,0:T(8,128)(2,1)S(1)}, bf16[64,2560]{1,0:T(8,128)(2,1)}, u32[]{:S(2)}, u32[]{:S(2)}) %collective-permute-start.15) | collective-permute-done | bytes 327712 | tf_op jit(solution)/shard_map/ppermute | solution.py:13
  436.5 23.0 %collective-permute-done.21 = bf16[128,2560]{1,0:T(8,128)(2,1)} collective-permute-done((bf16[128,2560]{1,0:T(8,128)(2,1)S(1)}, bf16[128,2560]{1,0:T(8,128)(2,1)}, u32[]{:S(2)}, u32[]{:S(2)}) %collective-permute-start.21) | collective-permute-done | bytes 655392 | tf_op jit(solution)/shard_map/ppermute | solution.py:21
  461.7 9.0 %collective-permute-done.22 = bf16[64,2560]{1,0:T(8,128)(2,1)S(1)} collective-permute-done((bf16[64,2560]{1,0:T(8,128)(2,1)S(1)}, bf16[64,2560]{1,0:T(8,128)(2,1)S(1)}, u32[]{:S(2)}, u32[]{:S(2)}) %collective-permute-start.22) | collective-permute-done | bytes 327712 | tf_op jit(solution)/shard_map/ppermute | solution.py:13
  (158 shorter events, 104.7 us)
Async XLA Ops:
  0.0 13.5 %collective-permute-start = (s32[2,64,2]{1,2,0:T(2,128)}, s32[2,64,2]{1,2,0:T(2,128)S(1)}, u32[]{:S(2)}, u32[]{:S(2)}) collective-permute-start(s32[2,64,2]{1,2,0:T(2,128)} %param.13), channel_id=1, source_target_pairs={{0,16},{16,0},{1,17},{17,1},{2,18},{18,2},{3,19},{19,3},{4,20},{20... | collective-permute-start | bytes 3080 | tf_op jit(solution)/shard_map/ppermute | solution.py:13
  8.2 18.1 %all-to-all-start = ((bf16[32,2,2560]{2,1,0:T(2,128)(2,1)}), bf16[32,2,2560]{2,1,0:T(2,128)(2,1)S(1)}, u32[]{:S(2)}, u32[]{:S(2)}) async-start(bf16[32,2,2560]{2,1,0:T(2,128)(2,1)} %reshape.287), calls=%async_computation | async-start | bytes 655360 | tf_op jit(solution)/shard_map/all_to_all | solution.py:38
  13.6 10.5 %collective-permute-start.1 = (s32[2,2,64,2]{2,3,1,0:T(2,128)S(1)}, s32[2,2,64,2]{2,3,1,0:T(2,128)S(1)}, u32[]{:S(2)}, u32[]{:S(2)}) collective-permute-start(s32[2,2,64,2]{2,3,1,0:T(2,128)S(1)} %get-tuple-element.34), channel_id=1, source_target_pairs={{0,4},{4,0},{1,5},{5,1},{2,6},{6,2},{3,7},{7,3},{8,12},{12,8},{9,1... | collective-permute-start | bytes 6152 | tf_op jit(solution)/shard_map/ppermute | solution.py:21
  27.1 37.7 %all-to-all-start.1 = ((bf16[8,16,5120]{2,1,0:T(8,128)(2,1)}), bf16[8,16,5120]{2,1,0:T(8,128)(2,1)S(1)}, u32[]{:S(2)}, u32[]{:S(2)}) async-start(bf16[8,16,5120]{2,1,0:T(8,128)(2,1)} %fusion.34), calls=%async_computation.1 | async-start | bytes 2621440 | tf_op jit(solution)/shard_map/all_to_all | solution.py:143
  30.7 32.1 %collective-permute-start.11 = (bf16[64,5120]{1,0:T(8,128)(2,1)S(1)}, bf16[64,5120]{1,0:T(8,128)(2,1)S(1)}, u32[]{:S(2)}, u32[]{:S(2)}) collective-permute-start(bf16[64,5120]{1,0:T(8,128)(2,1)S(1)} %get-tuple-element.21), channel_id=1, source_target_pairs={{0,4},{4,0},{1,5},{5,1},{2,6},{6,2},{3,7},{7,3},{8,12},{12,8},{9,1... | collective-permute-start | bytes 1966088 | tf_op jit(solution)/shard_map/ppermute | solution.py:21
  64.8 24.1 %all-to-all-start.3 = ((bf16[8,16,5120]{2,1,0:T(8,128)(2,1)}), bf16[8,16,5120]{2,1,0:T(8,128)(2,1)}, u32[]{:S(2)}, u32[]{:S(2)}) async-start(bf16[8,16,5120]{2,1,0:T(8,128)(2,1)} %fusion.32), calls=%async_computation.3 | async-start | bytes 2621440 | tf_op jit(solution)/shard_map/all_to_all | solution.py:143
  69.0 17.0 %collective-permute-start.16 = (bf16[64,5120]{1,0:T(8,128)(2,1)S(1)}, bf16[64,5120]{1,0:T(8,128)(2,1)S(1)}, u32[]{:S(2)}, u32[]{:S(2)}) collective-permute-start(bf16[64,5120]{1,0:T(8,128)(2,1)S(1)} %get-tuple-element.22), channel_id=1, source_target_pairs={{0,16},{16,0},{1,17},{17,1},{2,18},{18,2},{3,19},{19,3},{4,20},{20... | collective-permute-start | bytes 1966088 | tf_op jit(solution)/shard_map/ppermute | solution.py:13
  88.8 85.0 %all-to-all-start.5 = ((bf16[8,32,5120]{2,1,0:T(8,128)(2,1)}), bf16[8,32,5120]{2,1,0:T(8,128)(2,1)S(1)}, u32[]{:S(2)}, u32[]{:S(2)}) async-start(bf16[8,32,5120]{2,1,0:T(8,128)(2,1)} %fusion.13), calls=%async_computation.5 | async-start | bytes 5242880 | tf_op jit(solution)/shard_map/all_to_all | solution.py:136
  92.7 43.3 %collective-permute-start.18 = (bf16[64,5120]{1,0:T(8,128)(2,1)S(1)}, bf16[64,5120]{1,0:T(8,128)(2,1)}, u32[]{:S(2)}, u32[]{:S(2)}) collective-permute-start(bf16[64,5120]{1,0:T(8,128)(2,1)S(1)} %get-tuple-element.22), channel_id=1, source_target_pairs={{0,4},{4,0},{1,5},{5,1},{2,6},{6,2},{3,7},{7,3},{8,12},{12,8},{9,1... | collective-permute-start | bytes 1966088 | tf_op jit(solution)/shard_map/ppermute | solution.py:21
  100.0 138.9 %collective-permute-start.6 = (bf16[2,192,5120]{2,1,0:T(8,128)(2,1)}, bf16[2,192,5120]{2,1,0:T(8,128)(2,1)}, u32[]{:S(2)}, u32[]{:S(2)}) collective-permute-start(bf16[2,192,5120]{2,1,0:T(8,128)(2,1)} %get-tuple-element.20), channel_id=1, source_target_pairs={{0,8},{8,0},{1,9},{9,1},{2,10},{10,2},{3,11},{11,3},{4,12},{12,4},... | collective-permute-start | bytes 11796488 | tf_op jit(solution)/shard_map/ppermute | solution.py:17
  106.8 61.9 %collective-permute-start.9 = (bf16[2,192,2560]{2,1,0:T(8,128)(2,1)}, bf16[2,192,2560]{2,1,0:T(8,128)(2,1)}, u32[]{:S(2)}, u32[]{:S(2)}) collective-permute-start(bf16[2,192,2560]{2,1,0:T(8,128)(2,1)} %get-tuple-element.15), channel_id=1, source_target_pairs={{0,24},{8,16},{16,8},{24,0},{1,25},{9,17},{17,9},{25,1},{2,26},{10... | collective-permute-start | bytes 5898248 | tf_op jit(solution)/shard_map/ppermute | solution.py:25
  135.9 30.6 %collective-permute-start.19 = (bf16[64,5120]{1,0:T(8,128)(2,1)}, bf16[64,5120]{1,0:T(8,128)(2,1)S(1)}, u32[]{:S(2)}, u32[]{:S(2)}) collective-permute-start(bf16[64,5120]{1,0:T(8,128)(2,1)} %collective-permute-done.18), channel_id=1, source_target_pairs={{0,16},{16,0},{1,17},{17,1},{2,18},{18,2},{3,19},{19,3},{4,20},{20... | collective-permute-start | bytes 1966088 | tf_op jit(solution)/shard_map/ppermute | solution.py:13
  144.3 94.5 %collective-permute-start.5 = (bf16[2,192,5120]{2,1,0:T(8,128)(2,1)}, bf16[2,192,5120]{2,1,0:T(8,128)(2,1)}, u32[]{:S(2)}, u32[]{:S(2)}) collective-permute-start(bf16[2,192,5120]{2,1,0:T(8,128)(2,1)} %get-tuple-element.18), channel_id=1, source_target_pairs={{0,8},{8,0},{1,9},{9,1},{2,10},{10,2},{3,11},{11,3},{4,12},{12,4},... | collective-permute-start | bytes 11796488 | tf_op jit(solution)/shard_map/ppermute | solution.py:17
  144.3 64.5 %collective-permute-start.8 = (bf16[2,192,2560]{2,1,0:T(8,128)(2,1)}, bf16[2,192,2560]{2,1,0:T(8,128)(2,1)}, u32[]{:S(2)}, u32[]{:S(2)}) collective-permute-start(bf16[2,192,2560]{2,1,0:T(8,128)(2,1)} %get-tuple-element.16), channel_id=1, source_target_pairs={{0,16},{16,0},{1,17},{17,1},{2,18},{18,2},{3,19},{19,3},{4,20},{20... | collective-permute-start | bytes 5898248 | tf_op jit(solution)/shard_map/ppermute | solution.py:13
  166.6 42.2 %collective-permute-start.7 = (bf16[2,192,2560]{2,1,0:T(8,128)(2,1)}, bf16[2,192,2560]{2,1,0:T(8,128)(2,1)}, u32[]{:S(2)}, u32[]{:S(2)}) collective-permute-start(bf16[2,192,2560]{2,1,0:T(8,128)(2,1)} %get-tuple-element.14), channel_id=1, source_target_pairs={{0,8},{8,0},{1,9},{9,1},{2,10},{10,2},{3,11},{11,3},{4,12},{12,4},... | collective-permute-start | bytes 5898248 | tf_op jit(solution)/shard_map/ppermute | solution.py:17
  168.8 68.1 %collective-permute-start.4 = (bf16[8,16,5120]{2,1,0:T(8,128)(2,1)}, bf16[8,16,5120]{2,1,0:T(8,128)(2,1)}, u32[]{:S(2)}, u32[]{:S(2)}) collective-permute-start(bf16[8,16,5120]{2,1,0:T(8,128)(2,1)} %copy-done.5), channel_id=1, source_target_pairs={{0,16},{16,0},{1,17},{17,1},{2,18},{18,2},{3,19},{19,3},{4,20},{20... | collective-permute-start | bytes 3932168 | tf_op jit(solution)/shard_map/ppermute | solution.py:13
  175.3 99.1 %all-to-all-start.7 = ((bf16[8,32,5120]{2,1,0:T(8,128)(2,1)}), bf16[8,32,5120]{2,1,0:T(8,128)(2,1)}, u32[]{:S(2)}, u32[]{:S(2)}) async-start(bf16[8,32,5120]{2,1,0:T(8,128)(2,1)} %fusion.10), calls=%async_computation.7 | async-start | bytes 5242880 | tf_op jit(solution)/shard_map/all_to_all | solution.py:136
  215.6 63.0 %collective-permute-start.12 = (bf16[8,16,5120]{2,1,0:T(8,128)(2,1)}, bf16[8,16,5120]{2,1,0:T(8,128)(2,1)}, u32[]{:S(2)}, u32[]{:S(2)}) collective-permute-start(bf16[8,16,5120]{2,1,0:T(8,128)(2,1)} %all-to-all-done.3), channel_id=1, source_target_pairs={{0,16},{16,0},{1,17},{17,1},{2,18},{18,2},{3,19},{19,3},{4,20},{20... | collective-permute-start | bytes 3932168 | tf_op jit(solution)/shard_map/ppermute | solution.py:13
  261.8 6.9 %collective-permute-start.10 = (bf16[2,128,384]{2,1,0:T(8,128)(2,1)S(1)}, bf16[2,128,384]{2,1,0:T(8,128)(2,1)S(1)}, u32[]{:S(2)}, u32[]{:S(2)}) collective-permute-start(bf16[2,128,384]{2,1,0:T(8,128)(2,1)S(1)} %bitcast.222), channel_id=1, source_target_pairs={{0,16},{16,0},{1,17},{17,1},{2,18},{18,2},{3,19},{19,3},{4,20},{20... | collective-permute-start | bytes 589832 | tf_op jit(solution)/shard_map/ppermute | solution.py:13
  274.4 30.3 %all-to-all-start.2 = ((bf16[8,32,2560]{2,1,0:T(8,128)(2,1)}), bf16[8,32,2560]{2,1,0:T(8,128)(2,1)}, u32[]{:S(2)}, u32[]{:S(2)}) async-start(bf16[8,32,2560]{2,1,0:T(8,128)(2,1)} %bitcast.52), calls=%async_computation.2 | async-start | bytes 2621440 | tf_op jit(solution)/shard_map/all_to_all | solution.py:163
  291.7 7.3 %collective-permute-start.13 = (bf16[2,128,384]{2,1,0:T(8,128)(2,1)S(1)}, bf16[2,128,384]{2,1,0:T(8,128)(2,1)S(1)}, u32[]{:S(2)}, u32[]{:S(2)}) collective-permute-start(bf16[2,128,384]{2,1,0:T(8,128)(2,1)S(1)} %bitcast.221), channel_id=1, source_target_pairs={{0,16},{16,0},{1,17},{17,1},{2,18},{18,2},{3,19},{19,3},{4,20},{20... | collective-permute-start | bytes 589832 | tf_op jit(solution)/shard_map/ppermute | solution.py:13
  304.6 31.7 %all-to-all-start.4 = ((bf16[8,32,2560]{2,1,0:T(8,128)(2,1)}), bf16[8,32,2560]{2,1,0:T(8,128)(2,1)}, u32[]{:S(2)}, u32[]{:S(2)}) async-start(bf16[8,32,2560]{2,1,0:T(8,128)(2,1)} %bitcast.67), calls=%async_computation.4 | async-start | bytes 2621440 | tf_op jit(solution)/shard_map/all_to_all | solution.py:163
  323.1 7.5 %collective-permute-start.20 = (bf16[2,128,384]{2,1,0:T(8,128)(2,1)S(1)}, bf16[2,128,384]{2,1,0:T(8,128)(2,1)S(1)}, u32[]{:S(2)}, u32[]{:S(2)}) collective-permute-start(bf16[2,128,384]{2,1,0:T(8,128)(2,1)S(1)} %bitcast.219), channel_id=1, source_target_pairs={{0,16},{16,0},{1,17},{17,1},{2,18},{18,2},{3,19},{19,3},{4,20},{20... | collective-permute-start | bytes 589832 | tf_op jit(solution)/shard_map/ppermute | solution.py:13
  326.5 14.1 %collective-permute-start.2 = (bf16[2,64,32]{1,2,0:T(8,128)(2,1)S(1)}, bf16[2,64,32]{1,2,0:T(8,128)(2,1)S(1)}, u32[]{:S(2)}, u32[]{:S(2)}) collective-permute-start(bf16[2,64,32]{1,2,0:T(8,128)(2,1)S(1)} %get-tuple-element.32), channel_id=1, source_target_pairs={{0,16},{16,0},{1,17},{17,1},{2,18},{18,2},{3,19},{19,3},{4,20},{20... | collective-permute-start | bytes 24584 | tf_op jit(solution)/shard_map/ppermute | solution.py:13
  336.3 46.0 %all-to-all-start.8 = ((bf16[8,32,2560]{2,1,0:T(8,128)(2,1)}), bf16[8,32,2560]{2,1,0:T(8,128)(2,1)}, u32[]{:S(2)}, u32[]{:S(2)}) async-start(bf16[8,32,2560]{2,1,0:T(8,128)(2,1)} %bitcast.95), calls=%async_computation.8 | async-start | bytes 2621440 | tf_op jit(solution)/shard_map/all_to_all | solution.py:163
  340.6 15.8 %collective-permute-start.3 = (bf16[2,2,64,32]{2,3,1,0:T(8,128)(2,1)S(1)}, bf16[2,2,64,32]{2,3,1,0:T(8,128)(2,1)S(1)}, u32[]{:S(2)}, u32[]{:S(2)}) collective-permute-start(bf16[2,2,64,32]{2,3,1,0:T(8,128)(2,1)S(1)} %pad_maximum_fusion.7), channel_id=1, source_target_pairs={{0,4},{4,0},{1,5},{5,1},{2,6},{6,2},{3,7},{7,3},{8,12},{12,8},{9,1... | collective-permute-start | bytes 49160 | tf_op jit(solution)/shard_map/ppermute | solution.py:21
  369.9 6.8 %collective-permute-start.17 = (bf16[2,128,384]{2,1,0:T(8,128)(2,1)S(1)}, bf16[2,128,384]{2,1,0:T(8,128)(2,1)S(1)}, u32[]{:S(2)}, u32[]{:S(2)}) collective-permute-start(bf16[2,128,384]{2,1,0:T(8,128)(2,1)S(1)} %bitcast.220), channel_id=1, source_target_pairs={{0,16},{16,0},{1,17},{17,1},{2,18},{18,2},{3,19},{19,3},{4,20},{20... | collective-permute-start | bytes 589832 | tf_op jit(solution)/shard_map/ppermute | solution.py:13
  382.3 54.2 %all-to-all-start.6 = ((bf16[8,32,2560]{2,1,0:T(8,128)(2,1)}), bf16[8,32,2560]{2,1,0:T(8,128)(2,1)S(1)}, u32[]{:S(2)}, u32[]{:S(2)}) async-start(bf16[8,32,2560]{2,1,0:T(8,128)(2,1)} %bitcast.82), calls=%async_computation.6 | async-start | bytes 2621440 | tf_op jit(solution)/shard_map/all_to_all | solution.py:163
  391.0 32.2 %collective-permute-start.14 = (bf16[128,2560]{1,0:T(8,128)(2,1)S(1)}, bf16[128,2560]{1,0:T(8,128)(2,1)S(1)}, u32[]{:S(2)}, u32[]{:S(2)}) collective-permute-start(bf16[128,2560]{1,0:T(8,128)(2,1)S(1)} %convolution_convert_fusion.5), channel_id=1, source_target_pairs={{0,4},{4,0},{1,5},{5,1},{2,6},{6,2},{3,7},{7,3},{8,12},{12,8},{9,1... | collective-permute-start | bytes 1966088 | tf_op jit(solution)/shard_map/ppermute | solution.py:21
  426.0 9.5 %collective-permute-start.15 = (bf16[64,2560]{1,0:T(8,128)(2,1)S(1)}, bf16[64,2560]{1,0:T(8,128)(2,1)}, u32[]{:S(2)}, u32[]{:S(2)}) collective-permute-start(bf16[64,2560]{1,0:T(8,128)(2,1)S(1)} %slice.89), channel_id=1, source_target_pairs={{0,16},{16,0},{1,17},{17,1},{2,18},{18,2},{3,19},{19,3},{4,20},{20... | collective-permute-start | bytes 983048 | tf_op jit(solution)/shard_map/ppermute | solution.py:13
  429.3 30.3 %collective-permute-start.21 = (bf16[128,2560]{1,0:T(8,128)(2,1)S(1)}, bf16[128,2560]{1,0:T(8,128)(2,1)}, u32[]{:S(2)}, u32[]{:S(2)}) collective-permute-start(bf16[128,2560]{1,0:T(8,128)(2,1)S(1)} %convolution_convert_fusion.4), channel_id=1, source_target_pairs={{0,4},{4,0},{1,5},{5,1},{2,6},{6,2},{3,7},{7,3},{8,12},{12,8},{9,1... | collective-permute-start | bytes 1966088 | tf_op jit(solution)/shard_map/ppermute | solution.py:21
  461.1 9.7 %collective-permute-start.22 = (bf16[64,2560]{1,0:T(8,128)(2,1)S(1)}, bf16[64,2560]{1,0:T(8,128)(2,1)S(1)}, u32[]{:S(2)}, u32[]{:S(2)}) collective-permute-start(bf16[64,2560]{1,0:T(8,128)(2,1)S(1)} %slice.96), channel_id=1, source_target_pairs={{0,16},{16,0},{1,17},{17,1},{2,18},{18,2},{3,19},{19,3},{4,20},{20... | collective-permute-start | bytes 983048 | tf_op jit(solution)/shard_map/ppermute | solution.py:13
  (16 other events, 187.8 us)

commit v3 on v2

v3 whole, which is shorter than its diff:
```python
import jax
import jax.numpy as jnp
from jax import lax
from jax.experimental import pallas as pl
from jax.experimental.pallas import tpu as pltpu
from jax.sharding import Mesh, PartitionSpec as P

epsilon = 1e-05
contract = (((1,), (1,)), ((), ()))
swap = [(0, 1), (1, 0)]
group = ("core", "inner")
everywhere = ("side", "core", "far", "inner")
vmem_bytes = 48 * 2**20
lanes = 128


def side_swap(values):
    return lax.ppermute(values, "side", swap)


def core_swap(values):
    return lax.ppermute(values, "core", swap)


def far_swap(values):
    return lax.ppermute(values, "far", swap)


def cross_swap(values):
    return lax.ppermute(values, ("side", "core"), [(0, 3), (1, 2), (2, 1), (3, 0)])


def send(values):
    return lax.all_to_all(values, group, split_axis=0, concat_axis=0, tiled=True)


def tie(*values):
    return lax.optimization_barrier(values)


def normalise(rows, norm_gain):
    current = rows.astype(jnp.float32)
    inverse_rms = lax.rsqrt(jnp.mean(current * current, axis=-1, keepdims=True) + epsilon)
    return (current * inverse_rms * norm_gain).astype(jnp.bfloat16)


def hidden_kernel(place, inputs, router, gate_own, up_own, gate_got, up_got, hidden, score):
    def work(gate, up):
        rows = inputs[0]
        gate_part = lax.dot_general(rows, gate, contract, preferred_element_type=jnp.float32)
        up_part = lax.dot_general(rows, up, contract, preferred_element_type=jnp.float32)
        hidden[0, 0] = (gate_part / (1.0 + jnp.exp(-gate_part)) * up_part).astype(jnp.bfloat16)

    @pl.when(pl.program_id(1) == 0)
    def _():
        work(gate_own[0, 0], up_own[0, 0])
        logits = lax.dot_general(
            inputs[0], router[0], contract, preferred_element_type=jnp.float32
        )
        gated = (1.0 / (1.0 + jnp.exp(-logits[:, :1]))).astype(jnp.bfloat16)
        score[0] = jnp.broadcast_to(gated, score.shape[1:])

    @pl.when(pl.program_id(1) == 1)
    def _():
        work(gate_got[0], up_got[0])


def make_hidden(place, inputs, router, gate_proj, up_proj, gate_got, up_got):
    local, rows, width = inputs.shape
    part = gate_proj.shape[2]
    own = pl.BlockSpec((1, 1, part, width), lambda i, j, place: (place[0] * local + i, 0, 0, 0))
    got = pl.BlockSpec((1, part, width), lambda i, j, place: (i, 0, 0))
    return pl.pallas_call(
        hidden_kernel,
        grid_spec=pltpu.PrefetchScalarGridSpec(
            num_scalar_prefetch=1,
            grid=(local, 2),
            in_specs=[
                pl.BlockSpec((1, rows, width), lambda i, j, place: (i, 0, 0)),
                pl.BlockSpec((1, router.shape[1], width), lambda i, j, place: (i, 0, 0)),
                own,
                own,
                got,
                got,
            ],
            out_specs=[
                pl.BlockSpec((1, 1, rows, part), lambda i, j, place: (i, j, 0, 0)),
                pl.BlockSpec((1, rows, lanes), lambda i, j, place: (i, 0, 0)),
            ],
        ),
        out_shape=[
            jax.ShapeDtypeStruct((local, 2, rows, part), jnp.bfloat16),
            jax.ShapeDtypeStruct((local, rows, lanes), jnp.bfloat16),
        ],
        compiler_params=pltpu.CompilerParams(vmem_limit_bytes=vmem_bytes),
        cost_estimate=pl.CostEstimate(flops=1, bytes_accessed=1, transcendentals=0),
    )(place, inputs, router, gate_proj, up_proj, gate_got, up_got)


def result_kernel(
    place, hidden, other, score, down_own, down_core, down_side, down_cross, result
):
    middle = hidden.shape[2] // 2
    half = down_core.shape[2]

    def product(values, weights):
        return jnp.dot(values, weights, preferred_element_type=jnp.float32)

    low, high = pl.ds(0, middle), pl.ds(middle, middle)
    for here, there in ((low, high), (high, low)):
        total = product(hidden[0, 0, here, :], down_own[0, 0])
        total += product(hidden[0, 1, here, :], down_core[0])
        total += product(other[0, 0, there, :], down_side[0])
        total += product(other[0, 1, there, :], down_cross[0])
        gated = total * score[0, here, :1].astype(jnp.float32)
        result[0, here, :half] = gated.astype(jnp.bfloat16)
    result[0, :, half:] = score[0]


def make_result(place, hidden, other, score, down_proj, down_core, down_side, down_cross):
    local, parts, rows, part = hidden.shape
    half = down_core.shape[2]
    units = pl.BlockSpec((1, parts, rows, part), lambda i, place: (i, 0, 0, 0))
    got = pl.BlockSpec((1, part, half), lambda i, place: (i, 0, 0))
    return pl.pallas_call(
        result_kernel,
        grid_spec=pltpu.PrefetchScalarGridSpec(
            num_scalar_prefetch=1,
            grid=(local,),
            in_specs=[
                units,
                units,
                pl.BlockSpec((1, rows, lanes), lambda i, place: (i, 0, 0)),
                pl.BlockSpec(
                    (1, 1, part, half), lambda i, place: (place[0] * local + i, 0, 0, place[1])
                ),
                got,
                got,
                got,
            ],
            out_specs=pl.BlockSpec((1, rows, half + lanes), lambda i, place: (i, 0, 0)),
        ),
        out_shape=jax.ShapeDtypeStruct((local, rows, half + lanes), jnp.bfloat16),
        compiler_params=pltpu.CompilerParams(vmem_limit_bytes=vmem_bytes),
        cost_estimate=pl.CostEstimate(flops=1, bytes_accessed=1, transcendentals=0),
    )(place, hidden, other, score, down_proj, down_core, down_side, down_cross)


def on_device(activations, norm_gain, router_weight, gate_proj, up_proj, down_proj, expert_ids):
    steps, rows, width = activations.shape
    top = expert_ids.shape[2]
    cores, fars, inners = (lax.axis_size(name) for name in ("core", "far", "inner"))
    local = gate_proj.shape[0] // cores
    experts = gate_proj.shape[0] * fars * inners
    capacity = max(2, 2 * top * rows // experts)
    part = gate_proj.shape[2]
    half = width // 2
    side, core, far = (lax.axis_index(name) for name in ("side", "core", "far"))
    place = jnp.stack([core, side]).astype(jnp.int32)
    peers = cores * inners
    slots = local * capacity
    two = jnp.eye(2, dtype=jnp.bfloat16)
    near_half = (steps, rows, cores, local, fars, inners)
    lower = jnp.tril(jnp.ones((rows, rows), jnp.bfloat16), -1)

    def slots_of(ids):
        named = jnp.any(ids[..., None] == jnp.arange(experts, dtype=jnp.int32), axis=2)
        earlier = jnp.einsum(
            "rq,sqe->sre", lower, named.astype(jnp.bfloat16), preferred_element_type=jnp.float32
        )
        mine = lax.dynamic_index_in_dim(named.reshape(near_half), far, 4, keepdims=False)
        rank = lax.dynamic_index_in_dim(earlier.reshape(near_half), far, 4, keepdims=False)
        taken = mine[..., None] & (rank[..., None] == jnp.arange(capacity, dtype=jnp.float32))
        return jnp.moveaxis(taken, 3, 4).astype(jnp.bfloat16)

    def single(taken, source):
        pack = jnp.einsum("rcnlt->cnltr", taken).reshape(peers * slots, rows)
        return jnp.dot(pack, normalise(source, norm_gain)).reshape(peers, slots, width)

    def double(taken, source, other):
        pack = jnp.einsum("prcnlt,pq->cnqltpr", jnp.stack(taken), two)
        pack = pack.reshape(peers * 2 * slots, 2 * rows)
        stacked = jnp.concatenate([source, other], axis=0)
        return jnp.dot(pack, normalise(stacked, norm_gain)).reshape(peers, 2 * slots, width)

    def expert_block(weights, which_core):
        return lax.dynamic_slice_in_dim(weights, which_core * local, local, 0)[:, 0]

    def down_block(which_core, which_side, i=None):
        first, count = (0, local) if i is None else (i, 1)
        return lax.dynamic_slice(
            down_proj,
            (which_core * local + first, 0, 0, which_side * half),
            (count, 1, part, half),
        )[:, 0]

    first, second = activations[0], activations[1]

    own_taken = slots_of(expert_ids)
    side_ids = side_swap(expert_ids)
    first_side = side_swap(first)
    first_far = far_swap(first)
    second_own = send(single(own_taken[1], second))
    far_ids = far_swap(jnp.stack([expert_ids, side_ids]))
    side_blocks = down_block(core, 1 - side)
    down_side = [side_swap(side_blocks[:1])]
    side_taken = slots_of(side_ids)
    outgoing = double([own_taken[0], side_taken[0]], first, first_side)
    gate_send, up_send = expert_block(gate_proj, 1 - core), expert_block(up_proj, 1 - core)
    outgoing, second_own, first_far, far_ids, down_side[0], side_blocks, second, gate_send, up_send = tie(
        outgoing, second_own, first_far, far_ids, down_side[0], side_blocks, second, gate_send, up_send
    )

    first_own = send(outgoing)
    first_far_side = side_swap(first_far)
    second_far = far_swap(second)
    down_side.append(side_swap(side_blocks[1:]))
    gate_got, up_got = core_swap(gate_send), core_swap(up_send)
    far_taken = slots_of(far_ids[0])
    far_side_taken = slots_of(far_ids[1])
    outgoing = double([far_taken[0], far_side_taken[0]], first_far, first_far_side)
    cross_blocks = down_block(1 - core, 1 - side)
    column = router_weight.reshape(1, width)
    column_got = core_swap(column)
    pair = jnp.where(
        core == 0,
        jnp.concatenate([column, column_got]),
        jnp.concatenate([column_got, column]),
    )
    outgoing, first_own, second_far, down_side[1], gate_got, up_got, cross_blocks, pair = tie(
        outgoing, first_own, second_far, down_side[1], gate_got, up_got, cross_blocks, pair
    )

    first_relay = send(outgoing)
    second_far_side = side_swap(second_far)
    pair_got = side_swap(pair)
    router = jnp.where(side == core, pair, pair_got)
    router = jnp.broadcast_to(router[:, None], (local, 16, width))
    down_cross = [cross_swap(cross_blocks[:1])]
    outgoing = double([far_taken[1], far_side_taken[1]], second_far, second_far_side)
    core_blocks = down_block(1 - core, side)

    def start_experts(inputs):
        hidden, score = make_hidden(
            place, inputs.reshape(local, -1, width), router, gate_proj, up_proj, gate_got, up_got
        )
        return hidden, side_swap(hidden), score

    def finish_experts(hidden, other, score):
        result = make_result(
            place, hidden, other, score, down_proj, down_core, down_side, down_cross
        )
        result = result.reshape(local, 2, peers, capacity, half + lanes)
        return jnp.transpose(result, (2, 1, 0, 3, 4)).reshape(peers, 2 * slots, half + lanes)

    def mid(arrived):
        arrived = arrived.reshape(peers, 2, local, capacity, width)
        return jnp.transpose(arrived, (2, 1, 0, 3, 4))

    own_hidden = start_experts(mid(first_own))

    def adder(step, taken):
        taken = jnp.stack([each[step] for each in taken])
        return jnp.einsum("prcnlt,pq->prcnqlt", taken, two).reshape(
            2 * rows, peers * 2 * slots
        )

    own_adders = [adder(step, [own_taken, side_taken]) for step in range(steps)]
    far_adders = [adder(step, [far_taken, far_side_taken]) for step in range(steps)]
    outgoing, first_relay, down_cross[0], cross_blocks, core_blocks, own_hidden, router = tie(
        outgoing, first_relay, down_cross[0], cross_blocks, core_blocks, own_hidden, router
    )

    second_relay = send(outgoing)
    down_cross.append(cross_swap(cross_blocks[1:]))
    down_core = core_swap(core_blocks)
    down_side, down_cross = (jnp.concatenate(pieces, axis=0) for pieces in (down_side, down_cross))
    relay_hidden = start_experts(mid(first_relay))
    outgoing = jnp.concatenate(
        [finish_experts(*own_hidden), finish_experts(*relay_hidden)], axis=1
    )
    outgoing, second_relay, second_own, own_adders, far_adders = tie(
        outgoing, second_relay, second_own, own_adders, far_adders
    )

    first_back = send(outgoing)
    middle = peers // 2
    pieces = [side_swap(second_own[:middle])]
    relay_hidden = start_experts(mid(second_relay))
    relay_hidden, second_own = tie(relay_hidden, second_own)
    pieces.append(side_swap(second_own[middle:]))
    outgoing = finish_experts(*relay_hidden)
    outgoing, first_back, pieces[0] = tie(outgoing, first_back, pieces[0])

    def add(matrix, returned):
        return jnp.dot(
            matrix, returned.reshape(-1, half + lanes), preferred_element_type=jnp.float32
        )

    def to_far(sums):
        numerators, total = sums[:, :half].astype(jnp.bfloat16), sums[:, half:]
        whole = total.astype(jnp.bfloat16)
        rest = (total - whole.astype(jnp.float32)).astype(jnp.bfloat16)
        spot = jnp.arange(lanes) < lanes // 2
        return far_swap(jnp.concatenate([numerators, jnp.where(spot, whole, rest)], axis=1))

    def finish(near, received):
        received = received.astype(jnp.float32)
        total = near[:, half : half + 1] + received[:, half : half + 1] + received[:, -1:]
        mixture = ((near[:, :half] + received[:, :half]) / total).astype(jnp.bfloat16)
        return mixture[:rows], side_swap(mixture[rows:])

    def lay_out(own, received):
        low = jnp.where(side == 0, own, received)
        high = jnp.where(side == 0, received, own)
        return jnp.concatenate([low, high], axis=1)

    second_relay_back = send(outgoing)
    first_back = first_back.reshape(peers, 2, 2 * slots, half + lanes)
    first_received = to_far(add(far_adders[0], first_back[:, 1]))
    first_near = add(own_adders[0], first_back[:, 0])
    arrived = jnp.stack([second_own, jnp.concatenate(pieces, axis=0)])
    arrived = arrived.reshape(2, peers, local, capacity, width)
    outgoing = finish_experts(*start_experts(jnp.transpose(arrived, (2, 0, 1, 3, 4))))
    outgoing, second_relay_back, first_received, first_near = tie(
        outgoing, second_relay_back, first_received, first_near
    )

    second_own_back = send(outgoing)
    second_received = to_far(add(far_adders[1], second_relay_back))
    first_out = finish(first_near, first_received)
    second_own_back, first_out = tie(second_own_back, first_out)
    second_out = finish(add(own_adders[1], second_own_back), second_received)
    return jnp.stack([lay_out(*first_out), lay_out(*second_out)])


def solution(mesh):
    sections, columns = mesh.shape["section"], mesh.shape["expert"]
    split = Mesh(
        mesh.devices.reshape(2, sections // 2, 2, columns // 2),
        ("side", "core", "far", "inner"),
    )
    weights = P(None, ("far", "inner"), ("side", "core"), None)
    return jax.shard_map(
        on_device,
        mesh=split,
        in_specs=(
            P(None, everywhere, None),
            P(),
            P(None, everywhere),
            weights,
            weights,
            weights,
            P(None, everywhere, None),
        ),
        out_specs=P(None, everywhere, None),
        check_vma=False,
    )
```

time: 482 us -> 335 us (0.70); the launches traced: 472 us -> 334 us
  waiting for transfers between devices: 251 us -> 127 us
  Pallas kernels: 0 us -> 71.4 us
  matrix products: 79.8 us -> 16.3 us
  other arithmetic: 30.9 us -> 14.2 us
  starting transfers between devices: 68.2 us -> 60 us
    ppermute x6 -> x5, waiting for transfers between devices: 134 us -> 42.2 us  [far_swap(): return lax.ppermute(values, 'far', swap)]
    pallas_call x0 -> x8, Pallas kernels: none -> 71.4 us  [the longest x4 49.2 us: make_hidden(): pl.pallas_call(hidden_kernel, grid_spec=pltpu.PrefetchScalarGridSpec(num_...]
    dot_general x19 -> x12, matrix products: 79.8 us -> 16.3 us  [the longest x3 10 us: double(): jnp.dot(pack, normalise(stacked, norm_gain))]
    ppermute x13 -> x15, waiting for transfers between devices: 117 us -> 68.5 us  [side_swap(): return lax.ppermute(values, 'side', swap)]
    concatenate x2 -> x3, other arithmetic: 16.8 us -> 1.95 us  [the longest x1 1.85 us: on_device(): jnp.concatenate([finish_experts(*own_hidden), finish_experts(*relay_hidde...]
    all_to_all x9 -> x7, starting transfers between devices: 40.4 us -> 29.9 us  [send(): lax.all_to_all(values, group, split_axis=0, concat_axis=0, tiled=True)]
    slice x4 -> x16, local copies, waits for them, and re-layouts: 0.07 us -> 10.2 us  [the longest x1 2.22 us: on_device(): down_side = [side_swap(side_blocks[:1])]]
    ppermute x3 -> x4, waiting for transfers between devices: 0.01 us -> 6.19 us  [core_swap(): return lax.ppermute(values, 'core', swap)]
  transfers between devices with their start and end apart: 32 -> 33, of which waited for: 16 -> 15; matrix products, arithmetic and copies ran while one was open for 31% -> 20% of each run, Pallas kernels for 0% -> 21%
where the time goes in v3:
time: 335 us; the launch traced here: 334 us
  waiting for transfers between devices  127 us (38%)
  Pallas kernels  71.4 us (21%)
  starting transfers between devices  60 us (18%)
  local copies, waits for them, and re-layouts  44 us (13%)
  matrix products  16.3 us (5%)
  other arithmetic  14.2 us (4%)
    ppermute x15, waiting for transfers between devices, side_swap(): return lax.ppermute(values, 'side', swap)  68.5 us
    pallas_call x4, Pallas kernels, make_hidden(): pl.pallas_call(hidden_kernel, grid_spec=pltpu.PrefetchScalarGridSpec(num_...  49.2 us
    ppermute x5, waiting for transfers between devices, far_swap(): return lax.ppermute(values, 'far', swap)  42.2 us
    all_to_all x7, starting transfers between devices, send(): lax.all_to_all(values, group, split_axis=0, concat_axis=0, tiled=True)  29.9 us
    pallas_call x4, Pallas kernels, make_result(): pl.pallas_call(result_kernel, grid_spec=pltpu.PrefetchScalarGridSpec(num_...  22.1 us
    ppermute x15, starting transfers between devices, side_swap(): return lax.ppermute(values, 'side', swap)  17.1 us
    ppermute x5, starting transfers between devices, far_swap(): return lax.ppermute(values, 'far', swap)  10.1 us
    dot_general x3, matrix products, double(): jnp.dot(pack, normalise(stacked, norm_gain))  10 us
  transfers between devices with their start and end apart: 33, of which 15 were waited for; matrix products, arithmetic and copies ran while one was open for 20% of the time, Pallas kernels for 21%

profile of v3, /device:TPU:0, one launch (start us, length us, event | category | flops | bytes accessed | tf_op | source)
XLA Modules:
  0.0 333.8 jit_solution(11165413638546459058)
XLA Ops:
  2.5 4.0 %collective-permute-start.2 = (bf16[64,5120]{1,0:T(8,128)(2,1)}, bf16[64,5120]{1,0:T(8,128)(2,1)}, u32[]{:S(2)}, u32[]{:S(2)}) collective-permute-start(bf16[64,5120]{1,0:T(8,128)(2,1)} %get-tuple-element.121), channel_id=1, source_target_pairs={{0,4},{4,0},{1,5},{5,1},{2,6},{6,2},{3,7},{7,3},{8,12},{12,8},{9,1... | collective-permute-start | bytes 1966088 | tf_op jit(solution)/shard_map/ppermute | solution.py:26
  14.5 3.8 %all-to-all-start = ((bf16[8,16,5120]{2,1,0:T(8,128)(2,1)}), bf16[8,16,5120]{2,1,0:T(8,128)(2,1)S(1)}, u32[]{:S(2)}, u32[]{:S(2)}) async-start(bf16[8,16,5120]{2,1,0:T(8,128)(2,1)} %fusion.29), calls=%async_computation | async-start | bytes 2621440 | tf_op jit(solution)/shard_map/all_to_all | solution.py:34
  18.3 4.2 %dynamic-slice_bitcast_fusion.1 = bf16[2,192,5120]{2,1,0:T(8,128)(2,1)} fusion(bf16[4,1,192,5120]{3,2,1,0:T(8,128)(2,1)} %gate_own.7, s32[]{:T(128)S(6)} %select_n.84), kind=kLoop, calls=%fused_computation.1 | loop fusion | bytes 7864324 | tf_op jit(solution)/shard_map/squeeze | solution.py:187
  22.6 4.2 %dynamic-slice_bitcast_fusion = bf16[2,192,5120]{2,1,0:T(8,128)(2,1)} fusion(bf16[4,1,192,5120]{3,2,1,0:T(8,128)(2,1)} %up_own.7, s32[]{:T(128)S(6)} %select_n.84), kind=kLoop, calls=%fused_computation | loop fusion | bytes 7864324 | tf_op jit(solution)/shard_map/squeeze | solution.py:187
  26.8 5.2 %dynamic-slice_bitcast_fusion.2 = (bf16[2,192,2560]{2,1,0:T(8,128)(2,1)}, bf16[2,192,2560]{2,1,0:T(8,128)(2,1)S(1)}, bf16[2,192,2560]{2,1,0:T(8,128)(2,1)}) fusion(bf16[4,1,192,5120]{3,2,1,0:T(8,128)(2,1)} %down_own.7, s32[]{:T(128)S(6)} %select_n.84, s32[]{:T(128)S(6)} %select_n.87, s32[]{:T(128)S(6)} %select_n.83, s32[]{:T(128)S(6)} %select_n.82), kind=kLoop, calls=%fused_computation.19 | loop fusion | bytes 11796496 | tf_op jit(solution)/shard_map/squeeze | solution.py:191
  36.7 3.8 %fusion.16 = bf16[8,32,5120]{2,1,0:T(8,128)(2,1)} fusion(bf16[8,32,128]{2,1,0:T(8,128)(2,1)} %dot_general.80, f32[5120]{0:T(1024)} %param.8, f32[128]{0:T(128)S(1)} %add_rsqrt_fusion.3, bf16[64,5120]{1,0:T(8,128)(2,1)} %collective-permute-done.1, bf16[64,5120]{1,0:T(8,128)(2,1)} %get-tuple-element.121), kind=kOutput, calls=%fused_computation.27 | convolution fusion | flops 340131840 | bytes 4018688 | tf_op jit(solution)/shard_map/dot_general | solution.py:184
  44.1 5.1 %all-to-all-done = bf16[8,16,5120]{2,1,0:T(8,128)(2,1)S(1)} async-done(((bf16[8,16,5120]{2,1,0:T(8,128)(2,1)}), bf16[8,16,5120]{2,1,0:T(8,128)(2,1)S(1)}, u32[]{:S(2)}, u32[]{:S(2)}) %all-to-all-start) | async-done | bytes 1310752 | tf_op jit(solution)/shard_map/all_to_all | solution.py:34
  50.2 4.4 %all-to-all-start.1 = ((bf16[8,32,5120]{2,1,0:T(8,128)(2,1)}), bf16[8,32,5120]{2,1,0:T(8,128)(2,1)}, u32[]{:S(2)}, u32[]{:S(2)}) async-start(bf16[8,32,5120]{2,1,0:T(8,128)(2,1)} %fusion.16), calls=%async_computation.1 | async-start | bytes 5242880 | tf_op jit(solution)/shard_map/all_to_all | solution.py:34
  55.7 6.2 %collective-permute-done.10 = bf16[1,5120]{1,0:T(2,128)(2,1)S(1)} collective-permute-done((bf16[1,5120]{1,0:T(2,128)(2,1)S(1)}, bf16[1,5120]{1,0:T(2,128)(2,1)S(1)}, u32[]{:S(2)}, u32[]{:S(2)}) %collective-permute-start.10) | collective-permute-done | bytes 10272 | tf_op jit(solution)/shard_map/ppermute | solution.py:22
  68.9 11.6 %collective-permute-done.5 = bf16[64,5120]{1,0:T(8,128)(2,1)} collective-permute-done((bf16[64,5120]{1,0:T(8,128)(2,1)}, bf16[64,5120]{1,0:T(8,128)(2,1)}, u32[]{:S(2)}, u32[]{:S(2)}) %collective-permute-start.5) | collective-permute-done | bytes 655392 | tf_op jit(solution)/shard_map/ppermute | solution.py:18
  82.2 3.8 %fusion.13 = bf16[8,32,5120]{2,1,0:T(8,128)(2,1)} fusion(bf16[8,32,128]{2,1,0:T(8,128)(2,1)S(1)} %dot_general.91, f32[128]{0:T(128)S(1)} %add_rsqrt_fusion.1, f32[5120]{0:T(1024)S(1)} %copy-done.13, bf16[64,5120]{1,0:T(8,128)(2,1)} %collective-permute-done.5, bf16[64,5120]{1,0:T(8,128)(2,1)} %collective-permute-done.2), kind=kOutput, calls=%fused_computation.25 | convolution fusion | flops 340131840 | bytes 4018688 | tf_op jit(solution)/shard_map/dot_general | solution.py:184
  86.0 12.0 %collective-permute-done.6 = bf16[64,5120]{1,0:T(8,128)(2,1)S(1)} collective-permute-done((bf16[64,5120]{1,0:T(8,128)(2,1)}, bf16[64,5120]{1,0:T(8,128)(2,1)S(1)}, u32[]{:S(2)}, u32[]{:S(2)}) %collective-permute-start.6) | collective-permute-done | bytes 655392 | tf_op jit(solution)/shard_map/ppermute | solution.py:26
  100.8 4.6 %all-to-all-start.2 = ((bf16[8,32,5120]{2,1,0:T(8,128)(2,1)}), bf16[8,32,5120]{2,1,0:T(8,128)(2,1)}, u32[]{:S(2)}, u32[]{:S(2)}) async-start(bf16[8,32,5120]{2,1,0:T(8,128)(2,1)} %fusion.13), calls=%async_computation.2 | async-start | bytes 5242880 | tf_op jit(solution)/shard_map/all_to_all | solution.py:34
  110.6 12.3 %shard_map.73 = (bf16[2,2,128,192]{3,2,1,0:T(8,128)(2,1)S(1)}, bf16[2,128,128]{2,1,0:T(8,128)(2,1)S(1)}) custom-call(s32[2]{0:T(128)S(1)} %pad_add_fusion.1.place, bf16[2,128,5120]{2,1,0:T(8,128)(2,1)S(1)} %bitcast.180, bf16[2,16,5120]{2,1,0:T(8,128)(2,1)S(1)} %broadcast_in_dim.16.router, bf16[4,1,192,5120]{3,2,1,0:T(8,128)(2,1)} %gate_own.7, ...), custom_call_target="tpu_custom_call" | custom-call | flops 1 | bytes 1 | tf_op jit(solution)/shard_map/pallas_call | solution.py:73
  129.2 22.8 %collective-permute-done.14.other = bf16[2,2,128,192]{3,2,1,0:T(8,128)(2,1)S(1)} collective-permute-done((bf16[2,2,128,192]{3,2,1,0:T(8,128)(2,1)S(1)}, bf16[2,2,128,192]{3,2,1,0:T(8,128)(2,1)S(1)}, u32[]{:S(2)}, u32[]{:S(2)}) %collective-permute-start.14) | collective-permute-done | bytes 196640 | tf_op jit(solution)/shard_map/ppermute | solution.py:18
  152.9 4.5 %all-to-all-start.3 = ((bf16[8,32,5120]{2,1,0:T(8,128)(2,1)}), bf16[8,32,5120]{2,1,0:T(8,128)(2,1)}, u32[]{:S(2)}, u32[]{:S(2)}) async-start(bf16[8,32,5120]{2,1,0:T(8,128)(2,1)} %fusion.10), calls=%async_computation.3 | async-start | bytes 5242880 | tf_op jit(solution)/shard_map/all_to_all | solution.py:34
  166.2 12.3 %shard_map.75 = (bf16[2,2,128,192]{3,2,1,0:T(8,128)(2,1)S(1)}, bf16[2,128,128]{2,1,0:T(8,128)(2,1)S(1)}) custom-call(s32[2]{0:T(128)S(1)} %pad_add_fusion.1.place, bf16[2,128,5120]{2,1,0:T(8,128)(2,1)S(1)} %bitcast.182, bf16[2,16,5120]{2,1,0:T(8,128)(2,1)S(1)} %broadcast_in_dim.16.router, bf16[4,1,192,5120]{3,2,1,0:T(8,128)(2,1)} %gate_own.7, ...), custom_call_target="tpu_custom_call" | custom-call | flops 1 | bytes 1 | tf_op jit(solution)/shard_map/pallas_call | solution.py:73
  179.0 5.1 %collective-permute-done.16 = bf16[1,192,2560]{2,1,0:T(8,128)(2,1)S(1)} collective-permute-done((bf16[1,192,2560]{2,1,0:T(8,128)(2,1)S(1)}, bf16[1,192,2560]{2,1,0:T(8,128)(2,1)S(1)}, u32[]{:S(2)}, u32[]{:S(2)}) %collective-permute-start.16) | collective-permute-done | bytes 983072 | tf_op jit(solution)/shard_map/ppermute | solution.py:30
  184.1 5.8 %collective-permute-done.17.other = bf16[2,2,128,192]{3,2,1,0:T(8,128)(2,1)S(1)} collective-permute-done((bf16[2,2,128,192]{3,2,1,0:T(8,128)(2,1)S(1)}, bf16[2,2,128,192]{3,2,1,0:T(8,128)(2,1)S(1)}, u32[]{:S(2)}, u32[]{:S(2)}) %collective-permute-start.17) | collective-permute-done | bytes 196640 | tf_op jit(solution)/shard_map/ppermute | solution.py:18
  189.9 5.5 %shard_map.76 = bf16[2,128,2688]{2,1,0:T(8,128)(2,1)S(1)} custom-call(s32[2]{0:T(128)S(1)} %pad_add_fusion.1.place, bf16[2,2,128,192]{3,2,1,0:T(8,128)(2,1)S(1)} %get-tuple-element.86.hidden, bf16[2,2,128,192]{3,2,1,0:T(8,128)(2,1)S(1)} %collective-permute-done.17.other, bf16[2,128,128]{2,1,0:T(8,128)(2,1)S(1)} %get-tuple-element.87.score, ...), custom_call_target="tpu_custom_call" | custom-call | flops 1 | bytes 1 | tf_op jit(solution)/shard_map/pallas_call | solution.py:125
  195.5 5.5 %shard_map.74 = bf16[2,128,2688]{2,1,0:T(8,128)(2,1)S(1)} custom-call(s32[2]{0:T(128)S(1)} %pad_add_fusion.1.place, bf16[2,2,128,192]{3,2,1,0:T(8,128)(2,1)S(1)} %get-tuple-element.76.hidden, bf16[2,2,128,192]{3,2,1,0:T(8,128)(2,1)S(1)} %collective-permute-done.14.other, bf16[2,128,128]{2,1,0:T(8,128)(2,1)S(1)} %get-tuple-element.78.score, ...), custom_call_target="tpu_custom_call" | custom-call | flops 1 | bytes 1 | tf_op jit(solution)/shard_map/pallas_call | solution.py:125
  203.1 4.6 %all-to-all-start.4 = ((bf16[8,64,2688]{2,1,0:T(8,128)(2,1)}), bf16[8,64,2688]{2,1,0:T(8,128)(2,1)}, u32[]{:S(2)}, u32[]{:S(2)}) async-start(bf16[8,64,2688]{2,1,0:T(8,128)(2,1)} %pad_maximum_fusion), calls=%async_computation.4 | async-start | bytes 5505024 | tf_op jit(solution)/shard_map/all_to_all | solution.py:34
  212.6 12.3 %shard_map.77 = (bf16[2,2,128,192]{3,2,1,0:T(8,128)(2,1)S(1)}, bf16[2,128,128]{2,1,0:T(8,128)(2,1)S(1)}) custom-call(s32[2]{0:T(128)S(1)} %pad_add_fusion.1.place, bf16[2,128,5120]{2,1,0:T(8,128)(2,1)S(1)} %bitcast.183, bf16[2,16,5120]{2,1,0:T(8,128)(2,1)S(1)} %broadcast_in_dim.16.router, bf16[4,1,192,5120]{3,2,1,0:T(8,128)(2,1)} %gate_own.7, ...), custom_call_target="tpu_custom_call" | custom-call | flops 1 | bytes 1 | tf_op jit(solution)/shard_map/pallas_call | solution.py:73
  225.3 7.7 %collective-permute-done.18.other = bf16[2,2,128,192]{3,2,1,0:T(8,128)(2,1)S(1)} collective-permute-done((bf16[2,2,128,192]{3,2,1,0:T(8,128)(2,1)S(1)}, bf16[2,2,128,192]{3,2,1,0:T(8,128)(2,1)S(1)}, u32[]{:S(2)}, u32[]{:S(2)}) %collective-permute-start.18) | collective-permute-done | bytes 196640 | tf_op jit(solution)/shard_map/ppermute | solution.py:18
  234.3 5.5 %shard_map.78 = bf16[2,128,2688]{2,1,0:T(8,128)(2,1)S(1)} custom-call(s32[2]{0:T(128)S(1)} %pad_add_fusion.1.place, bf16[2,2,128,192]{3,2,1,0:T(8,128)(2,1)S(1)} %get-tuple-element.95.hidden, bf16[2,2,128,192]{3,2,1,0:T(8,128)(2,1)S(1)} %collective-permute-done.18.other, bf16[2,128,128]{2,1,0:T(8,128)(2,1)S(1)} %get-tuple-element.97.score, ...), custom_call_target="tpu_custom_call" | custom-call | flops 1 | bytes 1 | tf_op jit(solution)/shard_map/pallas_call | solution.py:125
  241.0 4.3 %all-to-all-start.5 = ((bf16[8,32,2688]{2,1,0:T(8,128)(2,1)}), bf16[8,32,2688]{2,1,0:T(8,128)(2,1)}, u32[]{:S(2)}, u32[]{:S(2)}) async-start(bf16[8,32,2688]{2,1,0:T(8,128)(2,1)} %bitcast.189), calls=%async_computation.5 | async-start | bytes 2752512 | tf_op jit(solution)/shard_map/all_to_all | solution.py:34
  252.4 12.3 %shard_map.79 = (bf16[2,2,128,192]{3,2,1,0:T(8,128)(2,1)S(1)}, bf16[2,128,128]{2,1,0:T(8,128)(2,1)S(1)}) custom-call(s32[2]{0:T(128)S(1)} %pad_add_fusion.1.place, bf16[2,128,5120]{2,1,0:T(8,128)(2,1)S(1)} %bitcast.181, bf16[2,16,5120]{2,1,0:T(8,128)(2,1)S(1)} %broadcast_in_dim.16.router, bf16[4,1,192,5120]{3,2,1,0:T(8,128)(2,1)} %gate_own.7, ...), custom_call_target="tpu_custom_call" | custom-call | flops 1 | bytes 1 | tf_op jit(solution)/shard_map/pallas_call | solution.py:73
  267.9 5.2 %collective-permute-done.21.other = bf16[2,2,128,192]{3,2,1,0:T(8,128)(2,1)S(1)} collective-permute-done((bf16[2,2,128,192]{3,2,1,0:T(8,128)(2,1)S(1)}, bf16[2,2,128,192]{3,2,1,0:T(8,128)(2,1)S(1)}, u32[]{:S(2)}, u32[]{:S(2)}) %collective-permute-start.21) | collective-permute-done | bytes 196640 | tf_op jit(solution)/shard_map/ppermute | solution.py:18
  273.0 5.5 %shard_map.80 = bf16[2,128,2688]{2,1,0:T(8,128)(2,1)S(1)} custom-call(s32[2]{0:T(128)S(1)} %pad_add_fusion.1.place, bf16[2,2,128,192]{3,2,1,0:T(8,128)(2,1)S(1)} %get-tuple-element.100.hidden, bf16[2,2,128,192]{3,2,1,0:T(8,128)(2,1)S(1)} %collective-permute-done.21.other, bf16[2,128,128]{2,1,0:T(8,128)(2,1)S(1)} %get-tuple-element.101.score, ...), custom_call_target="tpu_custom_call" | custom-call | flops 1 | bytes 1 | tf_op jit(solution)/shard_map/pallas_call | solution.py:125
  281.3 3.7 %all-to-all-start.6 = ((bf16[8,32,2688]{2,1,0:T(8,128)(2,1)}), bf16[8,32,2688]{2,1,0:T(8,128)(2,1)S(1)}, u32[]{:S(2)}, u32[]{:S(2)}) async-start(bf16[8,32,2688]{2,1,0:T(8,128)(2,1)} %bitcast.83), calls=%async_computation.6 | async-start | bytes 2752512 | tf_op jit(solution)/shard_map/all_to_all | solution.py:34
  292.1 28.7 %collective-permute-done.24 = bf16[128,2688]{1,0:T(8,128)(2,1)} collective-permute-done((bf16[128,2688]{1,0:T(8,128)(2,1)S(1)}, bf16[128,2688]{1,0:T(8,128)(2,1)}, u32[]{:S(2)}, u32[]{:S(2)}) %collective-permute-start.24) | collective-permute-done | bytes 688160 | tf_op jit(solution)/shard_map/ppermute | solution.py:26
  325.7 6.7 %collective-permute-done.25 = bf16[64,2560]{1,0:T(8,128)(2,1)S(1)} collective-permute-done((bf16[64,2560]{1,0:T(8,128)(2,1)S(1)}, bf16[64,2560]{1,0:T(8,128)(2,1)S(1)}, u32[]{:S(2)}, u32[]{:S(2)}) %collective-permute-start.25) | collective-permute-done | bytes 327712 | tf_op jit(solution)/shard_map/ppermute | solution.py:18
  (204 shorter events, 89.5 us)
Async XLA Ops:
  2.5 38.0 %collective-permute-start.2 = (bf16[64,5120]{1,0:T(8,128)(2,1)}, bf16[64,5120]{1,0:T(8,128)(2,1)}, u32[]{:S(2)}, u32[]{:S(2)}) collective-permute-start(bf16[64,5120]{1,0:T(8,128)(2,1)} %get-tuple-element.121), channel_id=1, source_target_pairs={{0,4},{4,0},{1,5},{5,1},{2,6},{6,2},{3,7},{7,3},{8,12},{12,8},{9,1... | collective-permute-start | bytes 1966088 | tf_op jit(solution)/shard_map/ppermute | solution.py:26
  6.5 28.6 %collective-permute-start.1 = (bf16[64,5120]{1,0:T(8,128)(2,1)}, bf16[64,5120]{1,0:T(8,128)(2,1)}, u32[]{:S(2)}, u32[]{:S(2)}) collective-permute-start(bf16[64,5120]{1,0:T(8,128)(2,1)} %get-tuple-element.121), channel_id=1, source_target_pairs={{0,16},{16,0},{1,17},{17,1},{2,18},{18,2},{3,19},{19,3},{4,20},{20... | collective-permute-start | bytes 1966088 | tf_op jit(solution)/shard_map/ppermute | solution.py:18
  8.0 24.7 %collective-permute-start = (s32[2,64,2]{1,2,0:T(2,128)S(1)}, s32[2,64,2]{1,2,0:T(2,128)S(1)}, u32[]{:S(2)}, u32[]{:S(2)}) collective-permute-start(s32[2,64,2]{1,2,0:T(2,128)S(1)} %copy-done.22), channel_id=1, source_target_pairs={{0,16},{16,0},{1,17},{17,1},{2,18},{18,2},{3,19},{19,3},{4,20},{20... | collective-permute-start | bytes 3080 | tf_op jit(solution)/shard_map/ppermute | solution.py:18
  10.8 33.4 %collective-permute-start.4 = (bf16[1,192,2560]{2,1,0:T(8,128)(2,1)}, bf16[1,192,2560]{2,1,0:T(8,128)(2,1)}, u32[]{:S(2)}, u32[]{:S(2)}) collective-permute-start(bf16[1,192,2560]{2,1,0:T(8,128)(2,1)} %dynamic-slice_bitcast_fusion.5), channel_id=1, source_target_pairs={{0,16},{16,0},{1,17},{17,1},{2,18},{18,2},{3,19},{19,3},{4,20},{20... | collective-permute-start | bytes 2949128 | tf_op jit(solution)/shard_map/ppermute | solution.py:18
  14.5 34.7 %all-to-all-start = ((bf16[8,16,5120]{2,1,0:T(8,128)(2,1)}), bf16[8,16,5120]{2,1,0:T(8,128)(2,1)S(1)}, u32[]{:S(2)}, u32[]{:S(2)}) async-start(bf16[8,16,5120]{2,1,0:T(8,128)(2,1)} %fusion.29), calls=%async_computation | async-start | bytes 2621440 | tf_op jit(solution)/shard_map/all_to_all | solution.py:34
  32.8 7.8 %collective-permute-start.3 = (s32[2,2,64,2]{2,3,1,0:T(2,128)S(1)}, s32[2,2,64,2]{2,3,1,0:T(2,128)S(1)}, u32[]{:S(2)}, u32[]{:S(2)}) collective-permute-start(s32[2,2,64,2]{2,3,1,0:T(2,128)S(1)} %pad_add_fusion), channel_id=1, source_target_pairs={{0,4},{4,0},{1,5},{5,1},{2,6},{6,2},{3,7},{7,3},{8,12},{12,8},{9,1... | collective-permute-start | bytes 6152 | tf_op jit(solution)/shard_map/ppermute | solution.py:26
  50.2 50.6 %all-to-all-start.1 = ((bf16[8,32,5120]{2,1,0:T(8,128)(2,1)}), bf16[8,32,5120]{2,1,0:T(8,128)(2,1)}, u32[]{:S(2)}, u32[]{:S(2)}) async-start(bf16[8,32,5120]{2,1,0:T(8,128)(2,1)} %fusion.16), calls=%async_computation.1 | async-start | bytes 5242880 | tf_op jit(solution)/shard_map/all_to_all | solution.py:34
  54.6 46.2 %collective-permute-start.8 = (bf16[2,192,5120]{2,1,0:T(8,128)(2,1)}, bf16[2,192,5120]{2,1,0:T(8,128)(2,1)}, u32[]{:S(2)}, u32[]{:S(2)}) collective-permute-start(bf16[2,192,5120]{2,1,0:T(8,128)(2,1)} %dynamic-slice_bitcast_fusion.1), channel_id=1, source_target_pairs={{0,8},{8,0},{1,9},{9,1},{2,10},{10,2},{3,11},{11,3},{4,12},{12,4},... | collective-permute-start | bytes 11796488 | tf_op jit(solution)/shard_map/ppermute | solution.py:22
  55.0 45.8 %collective-permute-start.9 = (bf16[2,192,5120]{2,1,0:T(8,128)(2,1)}, bf16[2,192,5120]{2,1,0:T(8,128)(2,1)}, u32[]{:S(2)}, u32[]{:S(2)}) collective-permute-start(bf16[2,192,5120]{2,1,0:T(8,128)(2,1)} %dynamic-slice_bitcast_fusion), channel_id=1, source_target_pairs={{0,8},{8,0},{1,9},{9,1},{2,10},{10,2},{3,11},{11,3},{4,12},{12,4},... | collective-permute-start | bytes 11796488 | tf_op jit(solution)/shard_map/ppermute | solution.py:22
  55.2 6.6 %collective-permute-start.10 = (bf16[1,5120]{1,0:T(2,128)(2,1)S(1)}, bf16[1,5120]{1,0:T(2,128)(2,1)S(1)}, u32[]{:S(2)}, u32[]{:S(2)}) collective-permute-start(bf16[1,5120]{1,0:T(2,128)(2,1)S(1)} %bitcast.196), channel_id=1, source_target_pairs={{0,8},{8,0},{1,9},{9,1},{2,10},{10,2},{3,11},{11,3},{4,12},{12,4},... | collective-permute-start | bytes 30728 | tf_op jit(solution)/shard_map/ppermute | solution.py:22
  62.5 35.4 %collective-permute-start.6 = (bf16[64,5120]{1,0:T(8,128)(2,1)}, bf16[64,5120]{1,0:T(8,128)(2,1)S(1)}, u32[]{:S(2)}, u32[]{:S(2)}) collective-permute-start(bf16[64,5120]{1,0:T(8,128)(2,1)} %get-tuple-element.63), channel_id=1, source_target_pairs={{0,4},{4,0},{1,5},{5,1},{2,6},{6,2},{3,7},{7,3},{8,12},{12,8},{9,1... | collective-permute-start | bytes 1966088 | tf_op jit(solution)/shard_map/ppermute | solution.py:26
  62.6 18.0 %collective-permute-start.5 = (bf16[64,5120]{1,0:T(8,128)(2,1)}, bf16[64,5120]{1,0:T(8,128)(2,1)}, u32[]{:S(2)}, u32[]{:S(2)}) collective-permute-start(bf16[64,5120]{1,0:T(8,128)(2,1)} %collective-permute-done.2), channel_id=1, source_target_pairs={{0,16},{16,0},{1,17},{17,1},{2,18},{18,2},{3,19},{19,3},{4,20},{20... | collective-permute-start | bytes 1966088 | tf_op jit(solution)/shard_map/ppermute | solution.py:18
  65.3 35.6 %collective-permute-start.7 = (bf16[1,192,2560]{2,1,0:T(8,128)(2,1)}, bf16[1,192,2560]{2,1,0:T(8,128)(2,1)}, u32[]{:S(2)}, u32[]{:S(2)}) collective-permute-start(bf16[1,192,2560]{2,1,0:T(8,128)(2,1)} %slice.141), channel_id=1, source_target_pairs={{0,16},{16,0},{1,17},{17,1},{2,18},{18,2},{3,19},{19,3},{4,20},{20... | collective-permute-start | bytes 2949128 | tf_op jit(solution)/shard_map/ppermute | solution.py:18
  100.8 51.1 %all-to-all-start.2 = ((bf16[8,32,5120]{2,1,0:T(8,128)(2,1)}), bf16[8,32,5120]{2,1,0:T(8,128)(2,1)}, u32[]{:S(2)}, u32[]{:S(2)}) async-start(bf16[8,32,5120]{2,1,0:T(8,128)(2,1)} %fusion.13), calls=%async_computation.2 | async-start | bytes 5242880 | tf_op jit(solution)/shard_map/all_to_all | solution.py:34
  108.7 17.7 %collective-permute-start.11 = (bf16[64,5120]{1,0:T(8,128)(2,1)S(1)}, bf16[64,5120]{1,0:T(8,128)(2,1)S(1)}, u32[]{:S(2)}, u32[]{:S(2)}) collective-permute-start(bf16[64,5120]{1,0:T(8,128)(2,1)S(1)} %collective-permute-done.6), channel_id=1, source_target_pairs={{0,16},{16,0},{1,17},{17,1},{2,18},{18,2},{3,19},{19,3},{4,20},{20... | collective-permute-start | bytes 1966088 | tf_op jit(solution)/shard_map/ppermute | solution.py:18
  110.4 41.5 %collective-permute-start.12 = (bf16[1,192,2560]{2,1,0:T(8,128)(2,1)S(1)}, bf16[1,192,2560]{2,1,0:T(8,128)(2,1)S(1)}, u32[]{:S(2)}, u32[]{:S(2)}) collective-permute-start(bf16[1,192,2560]{2,1,0:T(8,128)(2,1)S(1)} %slice.142), channel_id=1, source_target_pairs={{0,24},{8,16},{16,8},{24,0},{1,25},{9,17},{17,9},{25,1},{2,26},{10... | collective-permute-start | bytes 2949128 | tf_op jit(solution)/shard_map/ppermute | solution.py:30
  122.9 29.0 %collective-permute-start.14 = (bf16[2,2,128,192]{3,2,1,0:T(8,128)(2,1)S(1)}, bf16[2,2,128,192]{3,2,1,0:T(8,128)(2,1)S(1)}, u32[]{:S(2)}, u32[]{:S(2)}) collective-permute-start(bf16[2,2,128,192]{3,2,1,0:T(8,128)(2,1)S(1)} %get-tuple-element.76.hidden), channel_id=1, source_target_pairs={{0,16},{16,0},{1,17},{17,1},{2,18},{18,2},{3,19},{19,3},{4,20},{20... | collective-permute-start | bytes 589832 | tf_op jit(solution)/shard_map/ppermute | solution.py:18
  152.9 50.2 %all-to-all-start.3 = ((bf16[8,32,5120]{2,1,0:T(8,128)(2,1)}), bf16[8,32,5120]{2,1,0:T(8,128)(2,1)}, u32[]{:S(2)}, u32[]{:S(2)}) async-start(bf16[8,32,5120]{2,1,0:T(8,128)(2,1)} %fusion.10), calls=%async_computation.3 | async-start | bytes 5242880 | tf_op jit(solution)/shard_map/all_to_all | solution.py:34
  157.4 32.6 %collective-permute-start.15 = (bf16[2,192,2560]{2,1,0:T(8,128)(2,1)}, bf16[2,192,2560]{2,1,0:T(8,128)(2,1)}, u32[]{:S(2)}, u32[]{:S(2)}) collective-permute-start(bf16[2,192,2560]{2,1,0:T(8,128)(2,1)} %get-tuple-element.79), channel_id=1, source_target_pairs={{0,8},{8,0},{1,9},{9,1},{2,10},{10,2},{3,11},{11,3},{4,12},{12,4},... | collective-permute-start | bytes 5898248 | tf_op jit(solution)/shard_map/ppermute | solution.py:22
  160.2 23.9 %collective-permute-start.16 = (bf16[1,192,2560]{2,1,0:T(8,128)(2,1)S(1)}, bf16[1,192,2560]{2,1,0:T(8,128)(2,1)S(1)}, u32[]{:S(2)}, u32[]{:S(2)}) collective-permute-start(bf16[1,192,2560]{2,1,0:T(8,128)(2,1)S(1)} %slice.143), channel_id=1, source_target_pairs={{0,24},{8,16},{16,8},{24,0},{1,25},{9,17},{17,9},{25,1},{2,26},{10... | collective-permute-start | bytes 2949128 | tf_op jit(solution)/shard_map/ppermute | solution.py:30
  178.5 11.4 %collective-permute-start.17 = (bf16[2,2,128,192]{3,2,1,0:T(8,128)(2,1)S(1)}, bf16[2,2,128,192]{3,2,1,0:T(8,128)(2,1)S(1)}, u32[]{:S(2)}, u32[]{:S(2)}) collective-permute-start(bf16[2,2,128,192]{3,2,1,0:T(8,128)(2,1)S(1)} %get-tuple-element.86.hidden), channel_id=1, source_target_pairs={{0,16},{16,0},{1,17},{17,1},{2,18},{18,2},{3,19},{19,3},{4,20},{20... | collective-permute-start | bytes 589832 | tf_op jit(solution)/shard_map/ppermute | solution.py:18
  203.1 37.9 %all-to-all-start.4 = ((bf16[8,64,2688]{2,1,0:T(8,128)(2,1)}), bf16[8,64,2688]{2,1,0:T(8,128)(2,1)}, u32[]{:S(2)}, u32[]{:S(2)}) async-start(bf16[8,64,2688]{2,1,0:T(8,128)(2,1)} %pad_maximum_fusion), calls=%async_computation.4 | async-start | bytes 5505024 | tf_op jit(solution)/shard_map/all_to_all | solution.py:34
  208.9 32.1 %collective-permute-start.19 = (bf16[4,16,5120]{2,1,0:T(8,128)(2,1)S(1)}, bf16[4,16,5120]{2,1,0:T(8,128)(2,1)}, u32[]{:S(2)}, u32[]{:S(2)}) collective-permute-start(bf16[4,16,5120]{2,1,0:T(8,128)(2,1)S(1)} %slice.146), channel_id=1, source_target_pairs={{0,16},{16,0},{1,17},{17,1},{2,18},{18,2},{3,19},{19,3},{4,20},{20... | collective-permute-start | bytes 1966088 | tf_op jit(solution)/shard_map/ppermute | solution.py:18
  224.9 8.2 %collective-permute-start.18 = (bf16[2,2,128,192]{3,2,1,0:T(8,128)(2,1)S(1)}, bf16[2,2,128,192]{3,2,1,0:T(8,128)(2,1)S(1)}, u32[]{:S(2)}, u32[]{:S(2)}) collective-permute-start(bf16[2,2,128,192]{3,2,1,0:T(8,128)(2,1)S(1)} %get-tuple-element.95.hidden), channel_id=1, source_target_pairs={{0,16},{16,0},{1,17},{17,1},{2,18},{18,2},{3,19},{19,3},{4,20},{20... | collective-permute-start | bytes 589832 | tf_op jit(solution)/shard_map/ppermute | solution.py:18
  233.9 16.6 %collective-permute-start.20 = (bf16[4,16,5120]{2,1,0:T(8,128)(2,1)}, bf16[4,16,5120]{2,1,0:T(8,128)(2,1)}, u32[]{:S(2)}, u32[]{:S(2)}) collective-permute-start(bf16[4,16,5120]{2,1,0:T(8,128)(2,1)} %slice.147), channel_id=1, source_target_pairs={{0,16},{16,0},{1,17},{17,1},{2,18},{18,2},{3,19},{19,3},{4,20},{20... | collective-permute-start | bytes 1966088 | tf_op jit(solution)/shard_map/ppermute | solution.py:18
  241.0 40.3 %all-to-all-start.5 = ((bf16[8,32,2688]{2,1,0:T(8,128)(2,1)}), bf16[8,32,2688]{2,1,0:T(8,128)(2,1)}, u32[]{:S(2)}, u32[]{:S(2)}) async-start(bf16[8,32,2688]{2,1,0:T(8,128)(2,1)} %bitcast.189), calls=%async_computation.5 | async-start | bytes 2752512 | tf_op jit(solution)/shard_map/all_to_all | solution.py:34
  247.8 33.5 %collective-permute-start.22 = (bf16[128,2688]{1,0:T(8,128)(2,1)S(1)}, bf16[128,2688]{1,0:T(8,128)(2,1)S(1)}, u32[]{:S(2)}, u32[]{:S(2)}) collective-permute-start(bf16[128,2688]{1,0:T(8,128)(2,1)S(1)} %pad_maximum_fusion.9), channel_id=1, source_target_pairs={{0,4},{4,0},{1,5},{5,1},{2,6},{6,2},{3,7},{7,3},{8,12},{12,8},{9,1... | collective-permute-start | bytes 2064392 | tf_op jit(solution)/shard_map/ppermute | solution.py:26
  264.7 8.3 %collective-permute-start.21 = (bf16[2,2,128,192]{3,2,1,0:T(8,128)(2,1)S(1)}, bf16[2,2,128,192]{3,2,1,0:T(8,128)(2,1)S(1)}, u32[]{:S(2)}, u32[]{:S(2)}) collective-permute-start(bf16[2,2,128,192]{3,2,1,0:T(8,128)(2,1)S(1)} %get-tuple-element.100.hidden), channel_id=1, source_target_pairs={{0,16},{16,0},{1,17},{17,1},{2,18},{18,2},{3,19},{19,3},{4,20},{20... | collective-permute-start | bytes 589832 | tf_op jit(solution)/shard_map/ppermute | solution.py:18
  281.3 40.7 %all-to-all-start.6 = ((bf16[8,32,2688]{2,1,0:T(8,128)(2,1)}), bf16[8,32,2688]{2,1,0:T(8,128)(2,1)S(1)}, u32[]{:S(2)}, u32[]{:S(2)}) async-start(bf16[8,32,2688]{2,1,0:T(8,128)(2,1)} %bitcast.83), calls=%async_computation.6 | async-start | bytes 2752512 | tf_op jit(solution)/shard_map/all_to_all | solution.py:34
  286.9 33.9 %collective-permute-start.24 = (bf16[128,2688]{1,0:T(8,128)(2,1)S(1)}, bf16[128,2688]{1,0:T(8,128)(2,1)}, u32[]{:S(2)}, u32[]{:S(2)}) collective-permute-start(bf16[128,2688]{1,0:T(8,128)(2,1)S(1)} %pad_maximum_fusion.10), channel_id=1, source_target_pairs={{0,4},{4,0},{1,5},{5,1},{2,6},{6,2},{3,7},{7,3},{8,12},{12,8},{9,1... | collective-permute-start | bytes 2064392 | tf_op jit(solution)/shard_map/ppermute | solution.py:26
  290.4 31.6 %collective-permute-start.23 = (bf16[64,2560]{1,0:T(8,128)(2,1)S(1)}, bf16[64,2560]{1,0:T(8,128)(2,1)}, u32[]{:S(2)}, u32[]{:S(2)}) collective-permute-start(bf16[64,2560]{1,0:T(8,128)(2,1)S(1)} %get-tuple-element.126), channel_id=1, source_target_pairs={{0,16},{16,0},{1,17},{17,1},{2,18},{18,2},{3,19},{19,3},{4,20},{20... | collective-permute-start | bytes 983048 | tf_op jit(solution)/shard_map/ppermute | solution.py:18
  322.9 9.5 %collective-permute-start.25 = (bf16[64,2560]{1,0:T(8,128)(2,1)S(1)}, bf16[64,2560]{1,0:T(8,128)(2,1)S(1)}, u32[]{:S(2)}, u32[]{:S(2)}) collective-permute-start(bf16[64,2560]{1,0:T(8,128)(2,1)S(1)} %slice.194), channel_id=1, source_target_pairs={{0,16},{16,0},{1,17},{17,1},{2,18},{18,2},{3,19},{19,3},{4,20},{20... | collective-permute-start | bytes 983048 | tf_op jit(solution)/shard_map/ppermute | solution.py:18
  (24 other events, 288.4 us)
